TPU v7x, 32 devices: a whole 2x2x4 slice. The times are simulated.
32 devices in a mesh: tp: 4 (over y, core), ep: 8 (over z, x).
Axes of the slice: x: 2, y: 2, z: 4, core: 2. Of those that a mesh axis runs over, the one named last changes fastest.
Arguments:
- tokens: bfloat16 [128, 8192], P('ep'), may hold values from -6 to 6
- cotangent: bfloat16 [128, 8192], P('ep'), may hold values from -6 to 6
- w_gate: bfloat16 [1792, 8192], P(('tp', 'ep')), may hold values from -0.0625 to 0.0625
- w_up: bfloat16 [1792, 8192], P(('tp', 'ep')), may hold values from -0.0625 to 0.0625
- w_down: bfloat16 [1792, 8192], P(('tp', 'ep')), may hold values from -0.5 to 0.5
- neuron_expert: int32 [1792], P(('tp', 'ep')), may hold values from 0 to 15, as said below
- neuron_slot: int32 [1792], P(('tp', 'ep')), may hold values from 0 to 55, as said below
- choice_expert: int32 [128, 8], P('ep'), may hold values from 0 to 15, all different within a row; in each aligned block of 16 rows (0 to 15, 16 to 31, ...) at most 16 rows name the same one
- choice_weight: float32 [128, 8], P('ep'), may hold values from 0.02 to 0.3
Outputs:
- output: bfloat16 [128, 8192], P('ep', 'tp')
- d_tokens: bfloat16 [128, 8192], P('ep', 'tp')
- d_weight: float32 [128, 8], P('ep')
- d_gate_exp: bfloat16 [16, 224, 8192], P('ep', 'tp')
- d_up_exp: bfloat16 [16, 224, 8192], P('ep', 'tp')
- d_down_exp: bfloat16 [16, 224, 8192], P('ep', 'tp')
Inputs may be any that keep to these rules, and one draw needn't show every extreme that they name: `neuron_expert`: expert e belongs to ep index e // 2. Among the 56 neurons starting at any multiple of 56, at most 14 name experts of one ep index. `neuron_slot`: within each tp range of 448 neurons, the neurons of one expert have distinct slots. `choice_expert`: each row names 8 different experts; in each aligned block of 16 rows no expert is named more than 16 times.
All inputs are finite; a program needn't handle non-finite values.
Results may differ from a plain program's by a relative error of at most 0.018.
Values may be sent and summed in bfloat16 or wider, within the bound.
A program may use at most 128 MiB of HBM per device.

v0:
```python
import jax
import jax.numpy as jnp
from jax import lax
from jax.sharding import PartitionSpec as P

NL = 56
E_DEV = 2
TOPK = 8


def earlier_same(labels):
    count = labels.shape[0]
    row_iota = lax.broadcasted_iota(jnp.int32, (count, count), 0)
    col_iota = lax.broadcasted_iota(jnp.int32, (count, count), 1)
    same = (labels[:, None] == labels[None, :]) & (col_iota < row_iota)
    return jnp.sum(same.astype(jnp.int32), 1)


def slope_of(gate):
    sig = jax.nn.sigmoid(gate)
    return sig * (1.0 + gate * (1.0 - sig))


def source_table(matches):
    column = lax.broadcasted_iota(jnp.int32, matches.shape, 1)
    index = jnp.sum(jnp.where(matches, column, 0), 1)
    return (index, jnp.any(matches, 1))


def pick_rows(rows, index, filled):
    taken = jnp.take(rows, index, axis=0)
    return jnp.where(filled[:, None], taken, jnp.zeros_like(taken))


def dispatch(rows, width):
    part_width = width // lax.axis_size("tp")
    mine = lax.dynamic_slice_in_dim(rows, lax.axis_index("tp") * part_width, part_width, 2)
    moved = lax.all_to_all(mine, "ep", split_axis=0, concat_axis=0, tiled=True)
    return lax.all_gather(moved, "tp", axis=2, tiled=True)


def to_sources(terms, n_ep, tcap):
    shares = []
    for term in terms:
        share = lax.psum_scatter(term.astype(jnp.bfloat16), "tp", scatter_dimension=1, tiled=True)
        shares.append(share.reshape(n_ep, tcap, -1))
    stacked = jnp.stack(shares, 1).reshape(n_ep, E_DEV * tcap, -1)
    moved = lax.all_to_all(stacked, "ep", split_axis=0, concat_axis=0, tiled=True)
    return moved.reshape(-1, stacked.shape[2])


def body(
    tokens,
    cotangent,
    w_gate,
    w_up,
    w_down,
    neuron_expert,
    neuron_slot,
    choice_expert,
    choice_weight,
):
    n_ep = lax.axis_size("ep")
    n_tp = lax.axis_size("tp")
    width = tokens.shape[1]
    local_width = width // n_tp
    peer_slots = 2 * ((NL + n_ep - 1) // n_ep)
    capacity = n_ep * peer_slots // E_DEV
    owner = neuron_expert // E_DEV
    target = owner * peer_slots + earlier_same(owner)
    packing = target[None, :] == jnp.arange(n_ep * peer_slots, dtype=jnp.int32)[:, None]
    pack_index, pack_filled = source_table(packing)
    labels = neuron_expert % E_DEV * capacity + neuron_slot + 1
    packed_labels = jnp.sum(jnp.where(packing, labels[None, :], 0), 1)
    packed_labels = packed_labels.astype(jnp.float32).astype(jnp.bfloat16).reshape(n_ep, peer_slots)

    def pack(weight):
        return pick_rows(weight, pack_index, pack_filled).reshape(n_ep, peer_slots, width)

    got_gate, got_up, got_down, got_labels = (
        lax.all_to_all(pack(w_gate), "ep", split_axis=0, concat_axis=0, tiled=True),
        lax.all_to_all(pack(w_up), "ep", split_axis=0, concat_axis=0, tiled=True),
        lax.all_to_all(pack(w_down), "ep", split_axis=0, concat_axis=0, tiled=True),
        lax.all_to_all(packed_labels, "ep", split_axis=0, concat_axis=0, tiled=True),
    )
    slot_of = got_labels.reshape(-1).astype(jnp.int32) - 1
    placing = slot_of[None, :] == jnp.arange(E_DEV * capacity, dtype=jnp.int32)[:, None]
    place_index, place_filled = source_table(placing)

    def place(rows):
        return pick_rows(rows.reshape(-1, width), place_index, place_filled).reshape(
            E_DEV, capacity, width
        )

    gate_exp = place(got_gate)
    up_exp = place(got_up)
    down_exp = place(got_down)
    tok_dev = tokens.shape[0]
    chosen = choice_expert.reshape(-1)
    count = chosen.shape[0]
    experts_all = E_DEV * n_ep
    tcap = max(2, 2 * count // experts_all)
    slot_ids = chosen * tcap + earlier_same(chosen)
    matching = slot_ids[None, :] == jnp.arange(experts_all * tcap, dtype=jnp.int32)[:, None]
    choice_of_slot, slot_used = source_table(matching)
    send_x = pick_rows(tokens, choice_of_slot // TOPK, slot_used)
    send_x = send_x.reshape(n_ep, E_DEV * tcap, width)
    x_got = dispatch(send_x, width).reshape(n_ep, E_DEV, tcap, width)
    saved = []
    terms = []
    for local in range(E_DEV):
        x_rows = x_got[:, local].reshape(-1, width)
        gate = jnp.einsum("rd,hd->rh", x_rows, gate_exp[local], preferred_element_type=jnp.float32)
        upper = jnp.einsum("rd,hd->rh", x_rows, up_exp[local], preferred_element_type=jnp.float32)
        hidden = (jax.nn.silu(gate) * upper).astype(jnp.bfloat16)
        terms.append(jnp.dot(hidden, down_exp[local], preferred_element_type=jnp.float32))
        saved.append((x_rows, gate, upper, hidden))
    results = to_sources(terms, n_ep, tcap)
    per_choice = jnp.take(results, slot_ids, axis=0).astype(jnp.float32)
    weights = choice_weight.reshape(-1, 1)
    output = jnp.sum((weights * per_choice).reshape(tok_dev, TOPK, local_width), 1).astype(
        jnp.bfloat16
    )
    cot_local = lax.dynamic_slice_in_dim(
        cotangent, lax.axis_index("tp") * local_width, local_width, 1
    ).astype(jnp.float32)
    partial_value = jnp.sum(
        per_choice.reshape(tok_dev, TOPK, local_width) * cot_local[:, None, :], 2
    )
    d_weight = lax.psum(partial_value, "tp")
    slot_weight = jnp.take(choice_weight.reshape(-1), choice_of_slot, axis=0)
    slot_cot = jnp.take(cotangent, choice_of_slot // TOPK, axis=0).astype(jnp.float32)
    scaled_rows = (slot_weight[:, None] * slot_cot).astype(jnp.bfloat16)
    send_g = jnp.where(slot_used[:, None], scaled_rows, jnp.zeros_like(scaled_rows))
    send_g = send_g.reshape(n_ep, E_DEV * tcap, width)
    g_got = dispatch(send_g, width).reshape(n_ep, E_DEV, tcap, width)
    grad_gate = []
    grad_up = []
    grad_down = []
    back_terms = []
    for local in range(E_DEV):
        x_rows, gate, upper, hidden = saved[local]
        g_rows = g_got[:, local].reshape(-1, width)
        d_hidden = jnp.einsum(
            "rd,hd->rh", g_rows, down_exp[local], preferred_element_type=jnp.float32
        )
        grad_down.append(
            jnp.einsum("rh,rd->hd", hidden, g_rows, preferred_element_type=jnp.float32).astype(
                jnp.bfloat16
            )
        )
        d_gate_rows = (d_hidden * upper * slope_of(gate)).astype(jnp.bfloat16)
        d_up_rows = (d_hidden * jax.nn.silu(gate)).astype(jnp.bfloat16)
        grad_gate.append(
            jnp.einsum("rh,rd->hd", d_gate_rows, x_rows, preferred_element_type=jnp.float32).astype(
                jnp.bfloat16
            )
        )
        grad_up.append(
            jnp.einsum("rh,rd->hd", d_up_rows, x_rows, preferred_element_type=jnp.float32).astype(
                jnp.bfloat16
            )
        )
        term = jnp.dot(d_gate_rows, gate_exp[local], preferred_element_type=jnp.float32)
        term = term + jnp.dot(d_up_rows, up_exp[local], preferred_element_type=jnp.float32)
        back_terms.append(term)
    d_rows = to_sources(back_terms, n_ep, tcap)
    d_choice = jnp.take(d_rows, slot_ids, axis=0).astype(jnp.float32)
    d_tokens = jnp.sum(d_choice.reshape(tok_dev, TOPK, local_width), 1).astype(jnp.bfloat16)
    return (
        output,
        d_tokens,
        d_weight,
        jnp.stack(grad_gate, 0),
        jnp.stack(grad_up, 0),
        jnp.stack(grad_down, 0),
    )


def solution(mesh):
    in_specs = (
        P("ep", None),
        P("ep", None),
        P(("tp", "ep"), None),
        P(("tp", "ep"), None),
        P(("tp", "ep"), None),
        P(("tp", "ep")),
        P(("tp", "ep")),
        P("ep", None),
        P("ep", None),
    )
    out_specs = (
        P("ep", "tp"),
        P("ep", "tp"),
        P("ep", None),
        P("ep", "tp", None),
        P("ep", "tp", None),
        P("ep", "tp", None),
    )
    return jax.shard_map(body, mesh=mesh, in_specs=in_specs, out_specs=out_specs, check_vma=False)
```

profile of v0, /device:TPU:0, one launch (start us, length us, event | category | flops | bytes accessed | tf_op | source)
XLA Modules:
  0.0 465.6 jit_solution(11708436849965425156)
XLA Ops:
  9.0 7.3 %all-to-all-start.1 = ((bf16[8,1,14]{2,1,0:T(2,128)(2,1)}), bf16[8,1,14]{2,1,0:T(2,128)(2,1)S(1)}, u32[]{:S(2)}, u32[]{:S(2)}) async-start(bf16[8,1,14]{2,1,0:T(2,128)(2,1)} %convert_element_type.135), calls=%async_computation.1 | async-start | bytes 8192 | tf_op jit(solution)/shard_map/all_to_all | solution.py:84
  20.3 5.2 %gather_fusion.1 = bf16[256,8192]{1,0:T(8,128)(2,1)} fusion(bf16[16,8192]{1,0:T(8,128)(2,1)S(1)} %copy-done.3, s32[1024]{0:T(1024)S(1)} %pad_clamp_fusion.4), kind=kCustom, calls=%fused_computation.clone | custom fusion | bytes 8389632 | tf_op jit(solution)/shard_map/jit(_take)/gather | solution.py:31
  25.5 5.2 %gather_fusion.9 = bf16[256,8192]{1,0:T(8,128)(2,1)} fusion(bf16[16,8192]{1,0:T(8,128)(2,1)S(1)} %copy-done.2, s32[1024]{0:T(1024)S(1)} %pad_clamp_fusion.4), kind=kCustom, calls=%fused_computation.4.clone | custom fusion | bytes 8389632 | tf_op jit(solution)/shard_map/jit(_take)/gather | solution.py:132
  30.7 5.6 %fusion.8 = (bf16[256,8192]{1,0:T(8,128)(2,1)}, bf16[256,8192]{1,0:T(8,128)(2,1)S(1)}) fusion(bf16[256,8192]{1,0:T(8,128)(2,1)} %gather_fusion.9, f32[256]{0:T(256)S(1)} %and_select_fusion, pred[256]{0:T(512)(128)(4,1)S(1)} %get-tuple-element.38, pred[256]{0:T(512)(128)(4,1)S(1)} %fusion.32, bf16[256,8192]{1,0:T(8,128)(2,1)} %gather_fusion.1), kind=kLoop, calls=%fused_computation.30 | loop fusion | flops 14680064 | bytes 16778752 | tf_op jit(solution)/shard_map/jit(_where)/select_n | solution.py:134
  37.3 6.0 %all-to-all-start = ((bf16[8,32,2048]{2,1,0:T(8,128)(2,1)}), bf16[8,32,2048]{2,1,0:T(8,128)(2,1)}, u32[]{:S(2)}, u32[]{:S(2)}) async-start(bf16[8,32,2048]{2,1,0:T(8,128)(2,1)} %constant_dynamic-slice_fusion.1), calls=%async_computation | async-start | bytes 2097152 | tf_op jit(solution)/shard_map/all_to_all | solution.py:38
  54.7 14.1 %all-to-all-done = bf16[8,32,2048]{2,1,0:T(8,128)(2,1)} async-done(((bf16[8,32,2048]{2,1,0:T(8,128)(2,1)}), bf16[8,32,2048]{2,1,0:T(8,128)(2,1)}, u32[]{:S(2)}, u32[]{:S(2)}) %all-to-all-start) | async-done | bytes 1048608 | tf_op jit(solution)/shard_map/all_to_all | solution.py:38
  68.9 4.3 all-to-all-start.6
  73.1 4.8 %select_select_fusion.2 = (bf16[112,8192]{1,0:T(8,128)(2,1)}, bf16[112,8192]{1,0:T(8,128)(2,1)}, bf16[112,8192]{1,0:T(8,128)(2,1)}) fusion(bf16[112,8192]{1,0:T(8,128)(2,1)} %gather_fusion.6, pred[112]{0:T(512)(128)(4,1)S(1)} %compare_and_fusion.2, pred[112]{0:T(512)(128)(4,1)S(1)} %fusion.37, bf16[112,8192]{1,0:T(8,128)(2,1)} %gather_fusion.4, ...), kind=kLoop, calls=%fused_computation.36 | loop fusion | flops 5505024 | bytes 11010272 | tf_op jit(solution)/shard_map/jit(_where)/select_n | solution.py:32
  80.8 17.7 %all-to-all-done.6 = bf16[8,32,2048]{2,1,0:T(8,128)(2,1)} async-done(((bf16[8,32,2048]{2,1,0:T(8,128)(2,1)}), bf16[8,32,2048]{2,1,0:T(8,128)(2,1)}, u32[]{:S(2)}, u32[]{:S(2)}) %all-to-all-start.6) | async-done | bytes 1048608 | tf_op jit(solution)/shard_map/all_to_all | solution.py:38
  105.7 44.6 %all-to-all-done.2 = bf16[8,14,8192]{2,1,0:T(8,128)(2,1)S(1)} async-done(((bf16[8,14,8192]{2,1,0:T(8,128)(2,1)}), bf16[8,14,8192]{2,1,0:T(8,128)(2,1)S(1)}, u32[]{:S(2)}, u32[]{:S(2)}) %all-to-all-start.2) | async-done | bytes 1835040 | tf_op jit(solution)/shard_map/all_to_all | solution.py:81
  151.6 4.5 all-to-all-start.3
  159.0 44.9 %all-to-all-done.3 = bf16[8,14,8192]{2,1,0:T(8,128)(2,1)} async-done(((bf16[8,14,8192]{2,1,0:T(8,128)(2,1)}), bf16[8,14,8192]{2,1,0:T(8,128)(2,1)}, u32[]{:S(2)}, u32[]{:S(2)}) %all-to-all-start.3) | async-done | bytes 1835040 | tf_op jit(solution)/shard_map/all_to_all | solution.py:82
  203.9 4.4 all-to-all-start.4
  219.1 36.9 %all-to-all-done.4 = bf16[8,14,8192]{2,1,0:T(8,128)(2,1)} async-done(((bf16[8,14,8192]{2,1,0:T(8,128)(2,1)}), bf16[8,14,8192]{2,1,0:T(8,128)(2,1)}, u32[]{:S(2)}, u32[]{:S(2)}) %all-to-all-start.4) | async-done | bytes 1835040 | tf_op jit(solution)/shard_map/all_to_all | solution.py:83
  260.8 5.3 %select_select_fusion.1 = (bf16[112,8192]{1,0:T(8,128)(2,1)}, bf16[112,8192]{1,0:T(8,128)(2,1)}, bf16[112,8192]{1,0:T(8,128)(2,1)}) fusion(bf16[112,8192]{1,0:T(8,128)(2,1)} %gather_fusion.7, pred[112]{0:T(512)(128)(4,1)S(1)} %compare_and_fusion.1, pred[112]{0:T(512)(128)(4,1)S(1)} %fusion.34, bf16[112,8192]{1,0:T(8,128)(2,1)} %gather_fusion.5, ...), kind=kLoop, calls=%fused_computation.35 | loop fusion | flops 5505024 | bytes 11010272 | tf_op jit(solution)/shard_map/jit(_where)/select_n | solution.py:32
  272.0 4.1 fusion.42
  297.2 15.4 %reduce-scatter.9.cloned.1.call-done = bf16[128,2048]{1,0:T(8,128)(2,1)} async-done(((bf16[128,8192]{1,0:T(8,128)(2,1)}), bf16[128,2048]{1,0:T(8,128)(2,1)}) %reduce-scatter.9.cloned.1.call-update) | async-done | bytes 524304 | tf_op jit(solution)/shard_map/reduce_scatter | solution.py:45
  312.6 34.0 %reduce-scatter.11.cloned.1.call-done = bf16[128,2048]{1,0:T(8,128)(2,1)} async-done(((bf16[128,8192]{1,0:T(8,128)(2,1)}), bf16[128,2048]{1,0:T(8,128)(2,1)}) %reduce-scatter.11.cloned.1.call-update) | async-done | bytes 524304 | tf_op jit(solution)/shard_map/reduce_scatter | solution.py:45
  348.8 5.5 %all-to-all-start.7 = ((bf16[8,32,2048]{2,1,0:T(8,128)(2,1)}), bf16[8,32,2048]{2,1,0:T(8,128)(2,1)}, u32[]{:S(2)}, u32[]{:S(2)}) async-start(bf16[8,32,2048]{2,1,0:T(8,128)(2,1)} %bitcast.87), calls=%async_computation.11 | async-start | bytes 2097152 | tf_op jit(solution)/shard_map/all_to_all | solution.py:48
  364.2 16.2 %reduce-scatter.5.cloned.1.call-done = bf16[128,2048]{1,0:T(8,128)(2,1)} async-done(((bf16[128,8192]{1,0:T(8,128)(2,1)}), bf16[128,2048]{1,0:T(8,128)(2,1)}) %reduce-scatter.5.cloned.1.call-update) | async-done | bytes 524304 | tf_op jit(solution)/shard_map/reduce_scatter | solution.py:45
  380.4 34.0 %reduce-scatter.7.cloned.1.call-done = bf16[128,2048]{1,0:T(8,128)(2,1)} async-done(((bf16[128,8192]{1,0:T(8,128)(2,1)}), bf16[128,2048]{1,0:T(8,128)(2,1)}) %reduce-scatter.7.cloned.1.call-update) | async-done | bytes 524304 | tf_op jit(solution)/shard_map/reduce_scatter | solution.py:45
  416.8 5.5 %all-to-all-start.5 = ((bf16[8,32,2048]{2,1,0:T(8,128)(2,1)}), bf16[8,32,2048]{2,1,0:T(8,128)(2,1)S(1)}, u32[]{:S(2)}, u32[]{:S(2)}) async-start(bf16[8,32,2048]{2,1,0:T(8,128)(2,1)} %bitcast.8), calls=%async_computation.7 | async-start | bytes 2097152 | tf_op jit(solution)/shard_map/all_to_all | solution.py:48
  429.9 18.1 %all-to-all-done.5 = bf16[8,32,2048]{2,1,0:T(8,128)(2,1)S(1)} async-done(((bf16[8,32,2048]{2,1,0:T(8,128)(2,1)}), bf16[8,32,2048]{2,1,0:T(8,128)(2,1)S(1)}, u32[]{:S(2)}, u32[]{:S(2)}) %all-to-all-start.5) | async-done | bytes 1048608 | tf_op jit(solution)/shard_map/all_to_all | solution.py:48
  452.0 6.1 %psum.7 = f32[16,8]{1,0:T(8,128)S(1)} all-reduce(f32[16,8]{1,0:T(8,128)S(1)} %reduce_sum.95), channel_id=1, replica_groups=mesh['tp'=4,'ep'=8] {'tp'}, use_global_device_ids=true, to_apply=%region_16.21 | all-reduce | flops 128 | bytes 1024 | tf_op jit(solution)/shard_map/psum | solution.py:130
  (147 shorter events, 101.5 us)
Async XLA Ops:
  7.2 36.2 %copy-start = (bf16[56,8192]{1,0:T(8,128)(2,1)S(1)}, bf16[56,8192]{1,0:T(8,128)(2,1)}, u32[]{:S(2)}) copy-start(bf16[56,8192]{1,0:T(8,128)(2,1)} %param.19) | copy-start | bytes 2752516
  7.2 13.1 %copy-start.3 = (bf16[16,8192]{1,0:T(8,128)(2,1)S(1)}, bf16[16,8192]{1,0:T(8,128)(2,1)}, u32[]{:S(2)}) copy-start(bf16[16,8192]{1,0:T(8,128)(2,1)} %param.17) | copy-start | bytes 786436
  9.0 28.4 %all-to-all-start.1 = ((bf16[8,1,14]{2,1,0:T(2,128)(2,1)}), bf16[8,1,14]{2,1,0:T(2,128)(2,1)S(1)}, u32[]{:S(2)}, u32[]{:S(2)}) async-start(bf16[8,1,14]{2,1,0:T(2,128)(2,1)} %convert_element_type.135), calls=%async_computation.1 | async-start | bytes 8192 | tf_op jit(solution)/shard_map/all_to_all | solution.py:84
  20.3 5.2 %copy-start.2 = (bf16[16,8192]{1,0:T(8,128)(2,1)S(1)}, bf16[16,8192]{1,0:T(8,128)(2,1)}, u32[]{:S(2)}) copy-start(bf16[16,8192]{1,0:T(8,128)(2,1)} %param.18) | copy-start | bytes 786436
  37.3 31.5 %all-to-all-start = ((bf16[8,32,2048]{2,1,0:T(8,128)(2,1)}), bf16[8,32,2048]{2,1,0:T(8,128)(2,1)}, u32[]{:S(2)}, u32[]{:S(2)}) async-start(bf16[8,32,2048]{2,1,0:T(8,128)(2,1)} %constant_dynamic-slice_fusion.1), calls=%async_computation | async-start | bytes 2097152 | tf_op jit(solution)/shard_map/all_to_all | solution.py:38
  43.4 2.9 copy-start.4
  52.3 20.9 %copy-start.20 = (bf16[112,8192]{1,0:T(8,128)(2,1)S(1)}, bf16[112,8192]{1,0:T(8,128)(2,1)}, u32[]{:S(2)}) copy-start(bf16[112,8192]{1,0:T(8,128)(2,1)} %gather_fusion.2) | copy-start | bytes 5505028
  68.9 29.6 %all-to-all-start.6 = ((bf16[8,32,2048]{2,1,0:T(8,128)(2,1)}), bf16[8,32,2048]{2,1,0:T(8,128)(2,1)}, u32[]{:S(2)}, u32[]{:S(2)}) async-start(bf16[8,32,2048]{2,1,0:T(8,128)(2,1)} %constant_dynamic-slice_fusion), calls=%async_computation.8 | async-start | bytes 2097152 | tf_op jit(solution)/shard_map/all_to_all | solution.py:38
  98.5 51.8 %all-to-all-start.2 = ((bf16[8,14,8192]{2,1,0:T(8,128)(2,1)}), bf16[8,14,8192]{2,1,0:T(8,128)(2,1)S(1)}, u32[]{:S(2)}, u32[]{:S(2)}) async-start(bf16[8,14,8192]{2,1,0:T(8,128)(2,1)} %reshape.184), calls=%async_computation.2 | async-start | bytes 4194304 | tf_op jit(solution)/shard_map/all_to_all | solution.py:81
  102.1 164.0 %all-gather.3.cloned.1.call-start = ((), (), s32[]{:S(2)}) async-start(), calls=%async_computation.12 | async-start | bytes 5242880 | tf_op jit(solution)/shard_map/all_gather | solution.py:39
  151.6 52.3 %all-to-all-start.3 = ((bf16[8,14,8192]{2,1,0:T(8,128)(2,1)}), bf16[8,14,8192]{2,1,0:T(8,128)(2,1)}, u32[]{:S(2)}, u32[]{:S(2)}) async-start(bf16[8,14,8192]{2,1,0:T(8,128)(2,1)} %reshape.186), calls=%async_computation.3 | async-start | bytes 4194304 | tf_op jit(solution)/shard_map/all_to_all | solution.py:82
  203.9 52.1 %all-to-all-start.4 = ((bf16[8,14,8192]{2,1,0:T(8,128)(2,1)}), bf16[8,14,8192]{2,1,0:T(8,128)(2,1)}, u32[]{:S(2)}, u32[]{:S(2)}) async-start(bf16[8,14,8192]{2,1,0:T(8,128)(2,1)} %reshape.188), calls=%async_computation.4 | async-start | bytes 4194304 | tf_op jit(solution)/shard_map/all_to_all | solution.py:83
  208.3 63.7 %all-gather.5.cloned.1.call-start = ((), (), s32[]{:S(2)}) async-start(), calls=%async_computation.15 | async-start | bytes 5242880 | tf_op jit(solution)/shard_map/all_gather | solution.py:39
  209.0 103.6 %reduce-scatter.9.cloned.1.call-start = ((), (), s32[]{:S(2)}) async-start(), calls=%async_computation.16 | async-start | bytes 2621440 | tf_op jit(solution)/shard_map/reduce_scatter | solution.py:45
  272.0 4.1 copy-start.17
  276.1 3.0 copy-start.10
  281.9 64.6 %reduce-scatter.11.cloned.1.call-start = ((), (), s32[]{:S(2)}) async-start(), calls=%async_computation.17 | async-start | bytes 2621440 | tf_op jit(solution)/shard_map/reduce_scatter | solution.py:45
  282.0 3.0 copy-start.18
  290.3 90.2 %reduce-scatter.5.cloned.1.call-start = ((), (), s32[]{:S(2)}) async-start(), calls=%async_computation.13 | async-start | bytes 2621440 | tf_op jit(solution)/shard_map/reduce_scatter | solution.py:45
  293.8 120.5 %reduce-scatter.7.cloned.1.call-start = ((), (), s32[]{:S(2)}) async-start(), calls=%async_computation.14 | async-start | bytes 2621440 | tf_op jit(solution)/shard_map/reduce_scatter | solution.py:45
  348.8 67.9 %all-to-all-start.7 = ((bf16[8,32,2048]{2,1,0:T(8,128)(2,1)}), bf16[8,32,2048]{2,1,0:T(8,128)(2,1)}, u32[]{:S(2)}, u32[]{:S(2)}) async-start(bf16[8,32,2048]{2,1,0:T(8,128)(2,1)} %bitcast.87), calls=%async_computation.11 | async-start | bytes 2097152 | tf_op jit(solution)/shard_map/all_to_all | solution.py:48
  414.4 7.9 %copy-start.22 = (bf16[1,56,8192]{2,1,0:T(8,128)(2,1)S(1)}, bf16[1,56,8192]{2,1,0:T(8,128)(2,1)}, u32[]{:S(2)}) copy-start(bf16[1,56,8192]{2,1,0:T(8,128)(2,1)} %fusion.7) | copy-start | bytes 2752516
  416.8 31.3 %all-to-all-start.5 = ((bf16[8,32,2048]{2,1,0:T(8,128)(2,1)}), bf16[8,32,2048]{2,1,0:T(8,128)(2,1)S(1)}, u32[]{:S(2)}, u32[]{:S(2)}) async-start(bf16[8,32,2048]{2,1,0:T(8,128)(2,1)} %bitcast.8), calls=%async_computation.7 | async-start | bytes 2097152 | tf_op jit(solution)/shard_map/all_to_all | solution.py:48
  448.0 10.7 %copy-start.1 = (bf16[56,8192]{1,0:T(8,128)(2,1)S(1)}, bf16[56,8192]{1,0:T(8,128)(2,1)}, u32[]{:S(2)}) copy-start(bf16[56,8192]{1,0:T(8,128)(2,1)} %param.19) | copy-start | bytes 2752516
  (16 other events, 32.7 us)
Sparse Core Ops, SparseCore 0:
  104.5 35.8 all-gather.2
  210.7 35.8 all-gather.4
  282.1 30.4 reduce-scatter.8
  315.1 31.3 reduce-scatter.10
  348.9 31.4 reduce-scatter.4
  382.9 31.3 reduce-scatter.6
where the time goes:
time: 467 us; the launch traced here: 466 us
  waiting for transfers between devices  277 us (59%)
  local copies, waits for them, and re-layouts  69.9 us (15%)
  starting transfers between devices  41.5 us (9%)
  other arithmetic  28.7 us (6%)
  matrix products  27.4 us (6%)
  between operations  14.6 us (3%)
  blocking collectives  6.07 us (1%)
    reduce_scatter x4, waiting for transfers between devices, to_sources(): lax.psum_scatter(term.astype(jnp.bfloat16), 'tp', scatter_dimension=1, ti...  99.5 us
    all_to_all x1, waiting for transfers between devices, body(): lax.all_to_all(pack(w_up), 'ep', split_axis=0, concat_axis=0, tiled=True)  44.9 us
    all_to_all x1, waiting for transfers between devices, body(): lax.all_to_all(pack(w_gate), 'ep', split_axis=0, concat_axis=0, tiled=True)  44.6 us
    all_to_all x1, waiting for transfers between devices, body(): lax.all_to_all(pack(w_down), 'ep', split_axis=0, concat_axis=0, tiled=True)  36.9 us
    all_to_all x2, waiting for transfers between devices, dispatch(): moved = lax.all_to_all(mine, 'ep', split_axis=0, concat_axis=0, tiled=True)  31.9 us
    gather x7, local copies, waits for them, and re-layouts, pick_rows(): taken = jnp.take(rows, index, axis=0)  22.7 us
    all_to_all x2, waiting for transfers between devices, to_sources(): lax.all_to_all(stacked, 'ep', split_axis=0, concat_axis=0, tiled=True)  18.1 us
    all_to_all x2, starting transfers between devices, to_sources(): lax.all_to_all(stacked, 'ep', split_axis=0, concat_axis=0, tiled=True)  11 us
  transfers between devices with their start and end apart: 14, of which 10 were waited for; matrix products, arithmetic and copies ran while one was open for 22% of the time, Pallas kernels for 0%

commit v1 on v0

v1 whole, which is shorter than its diff:
```python
import jax
import jax.numpy as jnp
from jax import lax
from jax.sharding import PartitionSpec as P

E_DEV = 2


def body(tokens, cotangent, w_gate, w_up, w_down, neuron_expert, neuron_slot, choice_expert, choice_weight):
    n_ep = lax.axis_size("ep")
    experts = E_DEV * n_ep
    neurons = w_gate.shape[0]
    peer_slots = 2 * ((neurons + n_ep - 1) // n_ep)
    capacity = n_ep * peer_slots // E_DEV
    bf16, f32 = jnp.bfloat16, jnp.float32

    expert_ids = jnp.arange(experts, dtype=jnp.int32)
    named = choice_expert[:, :, None] == expert_ids[None, None, :]
    weight_local = jnp.sum(jnp.where(named, choice_weight[:, :, None], 0.0), 1)
    weight_all = lax.all_gather(weight_local, "ep", axis=0, tiled=True)
    x_all = lax.all_gather(tokens, "ep", axis=0, tiled=True)
    c_all = lax.all_gather(cotangent, "ep", axis=0, tiled=True)
    labels = neuron_expert * capacity + neuron_slot
    labels_all = lax.all_gather(labels, "ep", axis=0, tiled=True)

    def rows_by_tokens(rows, wide):
        return jnp.einsum("nd,td->nt", rows, wide, preferred_element_type=f32)

    gate = rows_by_tokens(w_gate, x_all)
    upper = rows_by_tokens(w_up, x_all)
    value = rows_by_tokens(w_down, c_all)
    weight = jnp.take(weight_all, neuron_expert, axis=1).T
    sig = jax.nn.sigmoid(gate)
    silu = gate * sig
    hidden = silu * upper
    d_hidden = weight * value
    scaled = (weight * hidden).astype(bf16)
    d_gate = (d_hidden * upper * (sig * (1.0 + gate * (1.0 - sig)))).astype(bf16)
    d_up = (d_hidden * silu).astype(bf16)

    factors = jnp.concatenate([scaled, d_gate, d_up], 1)
    factors_all = lax.all_gather(factors, "ep", axis=0, tiled=True)

    def from_neurons(factor, rows):
        return jnp.einsum("nt,nd->td", factor, rows, preferred_element_type=f32)

    output = from_neurons(scaled, w_down).astype(bf16)
    d_tokens = (from_neurons(d_gate, w_gate) + from_neurons(d_up, w_up)).astype(bf16)

    def to_owner(rows):
        part = lax.psum_scatter(rows, "tp", scatter_dimension=1, tiled=True)
        return lax.psum_scatter(part, "ep", scatter_dimension=0, tiled=True)

    output = to_owner(output)
    d_tokens = to_owner(d_tokens)

    member = (neuron_expert[:, None] == expert_ids[None, :]).astype(f32)
    per_expert = jnp.einsum(
        "nt,ne->te", hidden * value, member, preferred_element_type=f32, precision=lax.Precision.HIGHEST
    )
    per_expert = lax.psum(per_expert, ("tp", "ep"))
    mine = lax.dynamic_slice_in_dim(per_expert, lax.axis_index("ep") * tokens.shape[0], tokens.shape[0], 0)
    d_weight = jnp.sum(jnp.where(named, mine[:, None, :], 0.0), 2)

    slots = E_DEV * capacity
    slot_of = labels_all - lax.axis_index("ep") * slots
    placing = (jnp.arange(slots, dtype=jnp.int32)[:, None] == slot_of[None, :]).astype(bf16)
    placed = jnp.dot(placing, factors_all, preferred_element_type=f32).astype(bf16)
    count = x_all.shape[0]

    def gradient(index, wide):
        factor = placed[:, index * count : (index + 1) * count]
        grad = jnp.dot(factor, wide, preferred_element_type=f32).astype(bf16)
        return grad.reshape(E_DEV, capacity, -1)

    return output, d_tokens, d_weight, gradient(1, x_all), gradient(2, x_all), gradient(0, c_all)


def solution(mesh):
    in_specs = (
        P("ep", None),
        P("ep", None),
        P(("tp", "ep"), None),
        P(("tp", "ep"), None),
        P(("tp", "ep"), None),
        P(("tp", "ep")),
        P(("tp", "ep")),
        P("ep", None),
        P("ep", None),
    )
    out_specs = (
        P("ep", "tp"),
        P("ep", "tp"),
        P("ep", None),
        P("ep", "tp", None),
        P("ep", "tp", None),
        P("ep", "tp", None),
    )
    return jax.shard_map(body, mesh=mesh, in_specs=in_specs, out_specs=out_specs, check_vma=False)
```

time: 467 us -> 392 us (0.84)
  blocking collectives: 6.07 us -> 113 us
  local copies, waits for them, and re-layouts: 69.9 us -> 4.12 us
  starting transfers between devices: 41.5 us -> 0.24 us
  waiting for transfers between devices: 277 us -> 240 us
  other arithmetic: 28.7 us -> 1.7 us
  matrix products: 27.4 us -> 18.2 us
    all_to_all x8 -> x0, waiting for transfers between devices: 176 us -> none  [the longest x1 44.9 us: body(): lax.all_to_all(pack(w_up), 'ep', split_axis=0, concat_axis=0, tiled=True)]
    all_gather x2, waiting for transfers between devices: 0.02 us -> 94.8 us  [the longest x1 48.6 us: body(): x_all = lax.all_gather(tokens, 'ep', axis=0, tiled=True)]
    all_gather x0 -> x2, blocking collectives: none -> 61.5 us  [the longest x1 31 us: body(): factors_all = lax.all_gather(factors, 'ep', axis=0, tiled=True)]
    reduce_scatter x4, waiting for transfers between devices: 99.5 us -> 143 us  [the longest x2 116 us: to_owner(): return lax.psum_scatter(part, 'ep', scatter_dimension=0, tiled=True)]
    all_to_all x8 -> x0, starting transfers between devices: 41 us -> none  [the longest x2 11 us: to_sources(): lax.all_to_all(stacked, 'ep', split_axis=0, concat_axis=0, tiled=True)]
    psum x1, blocking collectives: 6.07 us -> 39.6 us  [body(): per_expert = lax.psum(per_expert, ('tp', 'ep'))]
    gather x11 -> x1, local copies, waits for them, and re-layouts: 33.5 us -> 0.61 us  [body(): weight = jnp.take(weight_all, neuron_expert, axis=1).T]
    select_n x9 -> x0, other arithmetic: 16.5 us -> none  [the longest x2 10.1 us: pick_rows(): return jnp.where(filled[:, None], taken, jnp.zeros_like(taken))]
  transfers between devices with their start and end apart: 14 -> 6, of which waited for: 10 -> 5; matrix products, arithmetic and copies ran while one was open for 22% -> 5% of each run, Pallas kernels for 0% -> 0%
where the time goes in v1:
time: 392 us; the launch traced here: 391 us
  waiting for transfers between devices  240 us (61%)
  blocking collectives  113 us (29%)
  matrix products  18.2 us (5%)
  between operations  14.9 us (4%)
  local copies, waits for them, and re-layouts  4.12 us (1%)
    reduce_scatter x2, waiting for transfers between devices, to_owner(): return lax.psum_scatter(part, 'ep', scatter_dimension=0, tiled=True)  116 us
    all_gather x1, waiting for transfers between devices, body(): x_all = lax.all_gather(tokens, 'ep', axis=0, tiled=True)  48.6 us
    all_gather x1, waiting for transfers between devices, body(): c_all = lax.all_gather(cotangent, 'ep', axis=0, tiled=True)  46.2 us
    psum x1, blocking collectives, body(): per_expert = lax.psum(per_expert, ('tp', 'ep'))  39.6 us
    all_gather x1, blocking collectives, body(): factors_all = lax.all_gather(factors, 'ep', axis=0, tiled=True)  31 us
    all_gather x1, blocking collectives, body(): weight_all = lax.all_gather(weight_local, 'ep', axis=0, tiled=True)  30.5 us
    reduce_scatter x2, waiting for transfers between devices, to_owner(): part = lax.psum_scatter(rows, 'tp', scatter_dimension=1, tiled=True)  27.6 us
    unnamed x1, blocking collectives  11.4 us
  transfers between devices with their start and end apart: 6, of which 5 were waited for; matrix products, arithmetic and copies ran while one was open for 5% of the time, Pallas kernels for 0%

profile of v1, /device:TPU:0, one launch (start us, length us, event | category | flops | bytes accessed | tf_op | source)
XLA Modules:
  0.0 391.3 jit_solution(11817994247466290667)
XLA Ops:
  7.2 0.7 all-gather.3.cloned.1.call-update
  8.0 0.7 all-gather.5.cloned.1.call-update
  8.7 0.8 copy.20
  9.5 0.8 copy.21
  10.2 1.2 dynamic-slice
  12.1 0.8 add_dynamic-update-slice_fusion
  13.6 48.6 %all-gather.3.cloned.1.call-done = bf16[128,8192]{1,0:T(8,128)(2,1)} async-done(((bf16[16,8192]{1,0:T(8,128)(2,1)}), bf16[128,8192]{1,0:T(8,128)(2,1)}) %all-gather.3.cloned.1.call-update) | async-done | bytes 2097168 | tf_op jit(solution)/shard_map/all_gather | solution.py:21
  62.2 2.8 fusion.12
  65.0 0.9 fusion.11
  65.9 46.2 %all-gather.5.cloned.1.call-done = bf16[128,8192]{1,0:T(8,128)(2,1)} async-done(((bf16[16,8192]{1,0:T(8,128)(2,1)}), bf16[128,8192]{1,0:T(8,128)(2,1)}) %all-gather.5.cloned.1.call-update) | async-done | bytes 2097168 | tf_op jit(solution)/shard_map/all_gather | solution.py:22
  112.1 2.4 fusion.13
  114.8 39.6 %psum.7 = f32[128,16]{1,0:T(8,128)S(1)} all-reduce(f32[128,16]{1,0:T(8,128)S(1)} %fusion.5), channel_id=1, replica_groups=mesh['tp'=4,'ep'=8] {'tp','ep'}, use_global_device_ids=true, to_apply=%region_5.6 | all-reduce | flops 2048 | bytes 16384 | tf_op jit(solution)/shard_map/psum | solution.py:61
  154.6 30.5 %all_gather.15 = f32[128,16]{1,0:T(8,128)S(1)} all-gather(f32[16,16]{1,0:T(8,128)S(1)} %get-tuple-element.13), channel_id=1, replica_groups=mesh['tp'=4,'ep'=8] {'ep'}, dimensions={0}, use_global_device_ids=true | all-gather | bytes 9216 | tf_op jit(solution)/shard_map/all_gather | solution.py:20
  185.8 2.0 convolution_convert_fusion
  188.0 2.0 fusion.14
  190.0 2.1 fusion
  192.1 27.6 %reduce-scatter.5.cloned.1.call-done = bf16[128,2048]{1,0:T(8,128)(2,1)} async-done(((bf16[128,8192]{1,0:T(8,128)(2,1)}), bf16[128,2048]{1,0:T(8,128)(2,1)}) %reduce-scatter.5.cloned.1.call-update) | async-done | bytes 524304 | tf_op jit(solution)/shard_map/reduce_scatter | solution.py:51
  219.8 11.4 %all-reduce = s32[448]{0:T(512)S(1)} all-reduce(s32[448]{0:T(512)S(1)} %get-tuple-element.17), channel_id=1, replica_groups=mesh['tp'=4,'ep'=8] {'ep'}, use_global_device_ids=true, to_apply=%add | all-reduce | flops 448 | bytes 3584
  231.2 31.0 %all_gather.19 = bf16[448,384]{1,0:T(8,128)(2,1)S(1)} all-gather(bf16[56,384]{1,0:T(8,128)(2,1)S(1)} %pad_maximum_fusion), channel_id=1, replica_groups=mesh['tp'=4,'ep'=8] {'ep'}, dimensions={0}, use_global_device_ids=true | all-gather | bytes 387072 | tf_op jit(solution)/shard_map/all_gather | solution.py:42
  263.1 1.9 convolution_convert_fusion.3
  264.9 1.9 convolution_convert_fusion.2
  266.8 1.9 convolution_convert_fusion.1
  268.7 50.7 %reduce-scatter.7.cloned.1.call-done = bf16[16,2048]{1,0:T(8,128)(2,1)} async-done(((bf16[128,2048]{1,0:T(8,128)(2,1)}), bf16[16,2048]{1,0:T(8,128)(2,1)}) %reduce-scatter.7.cloned.1.call-update) | async-done | bytes 65552 | tf_op jit(solution)/shard_map/reduce_scatter | solution.py:52
  319.4 65.0 %reduce-scatter.11.cloned.1.call-done = bf16[16,2048]{1,0:T(8,128)(2,1)} async-done(((bf16[128,2048]{1,0:T(8,128)(2,1)}), bf16[16,2048]{1,0:T(8,128)(2,1)}) %reduce-scatter.11.cloned.1.call-update) | async-done | bytes 65552 | tf_op jit(solution)/shard_map/reduce_scatter | solution.py:52
  (36 shorter events, 3.1 us)
Async XLA Ops:
  7.2 104.9 %copy-start = (bf16[56,8192]{1,0:T(8,128)(2,1)S(1)}, bf16[56,8192]{1,0:T(8,128)(2,1)}, u32[]{:S(2)}) copy-start(bf16[56,8192]{1,0:T(8,128)(2,1)} %param.13) | copy-start | bytes 2752516
  7.2 55.0 %all-gather.3.cloned.1.call-start = ((), (), s32[]{:S(2)}) async-start(), calls=%async_computation.4 | async-start | bytes 2359296 | tf_op jit(solution)/shard_map/all_gather | solution.py:21
  7.9 104.2 %all-gather.5.cloned.1.call-start = ((), (), s32[]{:S(2)}) async-start(), calls=%async_computation.7 | async-start | bytes 2359296 | tf_op jit(solution)/shard_map/all_gather | solution.py:22
  8.7 211.0 %reduce-scatter.5.cloned.1.call-start = ((), (), s32[]{:S(2)}) async-start(), calls=%async_computation.5 | async-start | bytes 2621440 | tf_op jit(solution)/shard_map/reduce_scatter | solution.py:51
  62.2 2.8 copy-start.1
  62.2 2.8 copy-start.3
  65.9 48.6 %copy-start.5 = (s32[56]{0:T(128)S(1)}, s32[56]{0:T(128)}, u32[]{:S(2)}) copy-start(s32[56]{0:T(128)} %param.14) | copy-start | bytes 676
  187.9 74.2 %reduce-scatter.9.cloned.1.call-start = ((), (), s32[]{:S(2)}) async-start(), calls=%async_computation.8 | async-start | bytes 2621440 | tf_op jit(solution)/shard_map/reduce_scatter | solution.py:51
  188.0 2.0 copy-start.4
  192.1 127.3 %reduce-scatter.7.cloned.1.call-start = ((), (), s32[]{:S(2)}) async-start(), calls=%async_computation.6 | async-start | bytes 589824 | tf_op jit(solution)/shard_map/reduce_scatter | solution.py:52
  219.7 164.7 %reduce-scatter.11.cloned.1.call-start = ((), (), s32[]{:S(2)}) async-start(), calls=%async_computation.9 | async-start | bytes 589824 | tf_op jit(solution)/shard_map/reduce_scatter | solution.py:52
  264.9 1.9 copy-start.2
Sparse Core Ops, SparseCore 0:
  10.1 51.9 all-gather.2
  64.3 47.7 all-gather.4
  188.0 31.6 reduce-scatter.4
  222.2 31.3 reduce-scatter.8
  257.4 61.9 reduce-scatter.6
  323.5 60.8 reduce-scatter.10

commit v2 on v1

v2 whole, which is shorter than its diff:
```python
import functools

import jax
import jax.numpy as jnp
from jax import lax
from jax.experimental import pallas as pl
from jax.experimental.pallas import tpu as pltpu
from jax.sharding import PartitionSpec as P

E_DEV = 2
CORES = 2
LANES = 128
PACK = 16
MESH = pl.DeviceIdType.MESH
BF16, F32 = jnp.bfloat16, jnp.float32


def grid_of(n_tp, n_ep):
    n_x = 1
    while 8 * n_x * n_x <= n_ep:
        n_x *= 2
    return n_tp // CORES, n_ep // n_x, n_x


def each(low, high, step):
    def run(i, carry):
        step(i)
        return carry

    if high - low == 1:
        step(low)
    elif high > low:
        lax.fori_loop(low, high, run, 0)


def dot(left, right, dims, precision=None):
    return lax.dot_general(left, right, (dims, ((), ())), precision=precision, preferred_element_type=F32)


def kernel(
    n_tp, n_ep, tok, cot, wg, wu, wd, we, member, pack, label,
    out, dtok, dwt, grad_gate, grad_up, grad_down,
    xs, cs, wa, fs, fr, sw, rw, rv, part, rc, ry, rx, rz, grads,
    s_z, s_x, s_y, s_c, r_ag, s_w, r_w, s_f, r_f, s_s, r_s, s_v, r_v,
    s_rc, r_rc, s_ry, r_ry, s_rx, r_rx, s_rz, r_rz, s_g,
):
    n_y, n_z, n_x = grid_of(n_tp, n_ep)
    t, p = lax.axis_index("tp"), lax.axis_index("ep")
    y, c = t // CORES, lax.rem(t, CORES)
    z, x = p // n_x, lax.rem(p, n_x)
    other = 1 - c
    rows, width = tok.shape
    count = n_ep * rows
    quarter = width // n_tp
    group = n_z * rows
    bufs = (xs, cs)

    def place(z_, x_):
        return x_ * n_z + z_

    def at(z_, x_):
        return (t, z_ * n_x + x_)

    def ep_peer(i):
        return lax.rem(p + 1 + i, n_ep)

    def place_of(p_):
        return place(p_ // n_x, lax.rem(p_, n_x))

    def copy(src, dst, send, recv, device):
        return pltpu.make_async_remote_copy(
            src_ref=src, dst_ref=dst, send_sem=send, recv_sem=recv, device_id=device, device_id_type=MESH
        )

    def got(dst, recv, device):
        copy(dst, dst, s_v.at[0], recv, device).wait_recv()

    here = place(z, x)

    def rows_at(i, size):
        return pl.ds(pl.multiple_of(i * size, size), size)

    def cols_at(q):
        return pl.ds(pl.multiple_of(q * quarter, LANES), quarter)

    def block(a, k, q):
        return bufs[a].at[rows_at(k, rows), cols_at(q)]

    def ranked(k):
        return place(lax.rem(z + n_z - lax.rem(k, n_z), n_z), lax.rem(x + k // n_z, n_x))

    def z_send(a, i):
        b = block(a, here, t)
        return copy(b, b, s_z.at[a, i], r_ag.at[a, here, t], at(lax.rem(z + 1 + i, n_z), x))

    def x_send(a, k, i):
        b = block(a, ranked(k), t)
        return copy(b, b, s_x.at[a, k, i], r_ag.at[a, ranked(k), t], at(z, lax.rem(x + 1 + i, n_x)))

    def y_send(a, k, i):
        b = block(a, ranked(k), t)
        to = lax.rem(y + 1 + i, n_y) * CORES + c
        return copy(b, b, s_y.at[a, k, i], r_ag.at[a, ranked(k), t], (to, p))

    def c_send(a, k, qy):
        q = qy * CORES + c
        b = block(a, ranked(k), q)
        return copy(b, b, s_c.at[a, k, qy], r_ag.at[a, ranked(k), q], (y * CORES + other, p))

    def arrived(a, k, q):
        got(block(a, ranked(k), q), r_ag.at[a, ranked(k), q], (y * CORES + other, p))

    def w_send(i):
        b = wa.at[rows_at(here, rows)]
        return copy(b, b, s_w.at[i], r_w.at[here], (t, ep_peer(i)))

    def f_send(i):
        to = ep_peer(i)
        return copy(fs.at[rows_at(to, PACK)], fr.at[rows_at(p, PACK)], s_f.at[i], r_f.at[p], (t, to))

    def s_send(i):
        to = ep_peer(i)
        return copy(sw.at[rows_at(place_of(to), rows)], rw.at[p], s_s.at[i], r_s.at[p], (t, to))

    def v_send(i):
        to = lax.rem(t + 1 + i, n_tp)
        return copy(rv.at[t], rv.at[t], s_v.at[i], r_v.at[t], (to, p))

    def rc_send(a, qy, g):
        src = part.at[a, qy * CORES + other, rows_at(g, group)]
        return copy(src, rc.at[a, qy, g], s_rc.at[a, qy, g], r_rc.at[a, qy, g], (y * CORES + other, p))

    def ry_send(a, i, g):
        to = lax.rem(y + 1 + i, n_y) * CORES + c
        src = part.at[a, to, rows_at(g, group)]
        return copy(src, ry.at[a, n_y - 2 - i, g], s_ry.at[a, i, g], r_ry.at[a, n_y - 2 - i, g], (to, p))

    def rx_send(a, i):
        to = lax.rem(x + 1 + i, n_x)
        src = part.at[a, t, rows_at(to, group)]
        return copy(src, rx.at[a, x], s_rx.at[a, i], r_rx.at[a, x], at(z, to))

    def rz_send(a, i):
        to = lax.rem(z + 1 + i, n_z)
        src = part.at[a, t, rows_at(place(to, x), rows)]
        return copy(src, rz.at[a, z], s_rz.at[a, i], r_rz.at[a, z], at(to, x))

    barrier = pltpu.get_barrier_semaphore()
    each(0, n_ep - 1, lambda i: pl.semaphore_signal(barrier, inc=1, device_id=(t, ep_peer(i)), device_id_type=MESH))
    each(
        0, n_tp - 1,
        lambda i: pl.semaphore_signal(barrier, inc=1, device_id=(lax.rem(t + 1 + i, n_tp), p), device_id_type=MESH),
    )
    xs[rows_at(here, rows)] = tok[...]
    cs[rows_at(here, rows)] = cot[...]
    wa[rows_at(here, rows)] = we[...]
    pl.semaphore_wait(barrier, n_ep - 1 + n_tp - 1)

    for a in range(2):
        each(0, n_z - 1, lambda i: z_send(a, i).start())
        each(0, n_x - 1, lambda i: x_send(a, 0, i).start())
    each(0, n_ep - 1, lambda i: w_send(i).start())

    def forward(a):
        def near(k):
            arrived(a, k, t)
            each(0, n_x - 1, lambda i: x_send(a, k, i).start())
            each(0, n_y - 1, lambda i: y_send(a, k, i).start())
            c_send(a, k, y).start()

        def far(k):
            arrived(a, k, t)
            each(0, n_y - 1, lambda i: y_send(a, k, i).start())
            c_send(a, k, y).start()

        each(1, n_z, near)
        each(n_z, n_ep, far)

    def across(a):
        def from_y(i):
            qy = lax.rem(y + 1 + i, n_y)

            def one(k):
                arrived(a, k, qy * CORES + c)
                c_send(a, k, qy).start()

            each(1, n_ep, one)

        each(0, n_y - 1, from_y)

    def finish(a):
        each(0, n_y, lambda qy: each(1, n_ep, lambda k: arrived(a, k, qy * CORES + other)))

    def rows_by_tokens(weight, wide):
        def step(q, total):
            return total + dot(weight[:, cols_at(q)], wide[:, cols_at(q)], ((1,), (1,)))

        return lax.fori_loop(0, n_tp, step, jnp.zeros((weight.shape[0], count), F32))

    step_cols = min(quarter, 512)

    def spread(a, pairs):
        def one(q):
            def chunk(j):
                at_cols = pl.ds(pl.multiple_of(q * quarter + j * step_cols, LANES), step_cols)
                total = None
                for factor, weight in pairs:
                    term = dot(factor, weight[:, at_cols], ((1,), (0,)))
                    total = term if total is None else total + term
                part[a, q, :, pl.ds(pl.multiple_of(j * step_cols, LANES), step_cols)] = total.astype(BF16)

            each(0, quarter // step_cols, chunk)

        def away(i):
            qy = lax.rem(y + 1 + i, n_y)
            one(qy * CORES + other)
            each(0, n_x, lambda g: rc_send(a, qy, lax.rem(x + 1 + g, n_x)).start())

        each(0, n_y, away)
        each(0, n_y, lambda i: one(lax.rem(y + 1 + i, n_y) * CORES + c))

    def add_into(a, q, base, ref):
        def some(j):
            span = rows_at(base + j, rows)
            part[a, q, span] = (
                part[a, q, span].astype(F32) + ref[rows_at(j, rows)].astype(F32)
            ).astype(BF16)

        each(0, ref.shape[0] // rows, some)

    def reduce_core(a):
        def one(gi):
            g = lax.rem(x + 1 + gi, n_x)

            def turn(i):
                qy = lax.rem(y + 1 + i, n_y)
                got(rc.at[a, qy, g], r_rc.at[a, qy, g], (y * CORES + other, p))
                add_into(a, qy * CORES + c, g * n_z, rc.at[a, qy, g])

            def send(i):
                turn(i)
                ry_send(a, i, g).start()

            each(0, n_y - 1, send)
            turn(n_y - 1)

        each(0, n_x, one)

    def reduce_y(a):
        def one(g):
            def add(i):
                qy = lax.rem(y + 1 + i, n_y)
                got(ry.at[a, i, g], r_ry.at[a, i, g], (qy * CORES + c, p))
                add_into(a, t, g * n_z, ry.at[a, i, g])

            each(0, n_y - 1, add)

        def send(i):
            one(lax.rem(x + 1 + i, n_x))
            rx_send(a, i).start()

        each(0, n_x - 1, send)
        one(x)

    def reduce_x(a):
        def add(i):
            from_x = lax.rem(x + 1 + i, n_x)
            got(rx.at[a, from_x], r_rx.at[a, from_x], at(z, from_x))
            add_into(a, t, x * n_z, rx.at[a, from_x])

        each(0, n_x - 1, add)
        each(0, n_z - 1, lambda i: rz_send(a, i).start())

    def reduce_z(a, result):
        total = part[a, t, rows_at(here, rows)].astype(F32)
        for i in range(n_z - 1):
            from_z = lax.rem(z + 1 + i, n_z)
            got(rz.at[a, from_z], r_rz.at[a, from_z], at(from_z, x))
            total = total + rz[a, from_z].astype(F32)
        result[...] = total.astype(BF16)

    exact = lax.Precision.HIGHEST
    forward(0)
    forward(1)
    across(0)
    finish(0)
    gate = rows_by_tokens(wg, xs)
    upper = rows_by_tokens(wu, xs)
    each(0, n_ep - 1, lambda i: got(wa.at[rows_at(place_of(ep_peer(i)), rows)], r_w.at[place_of(ep_peer(i))], (t, ep_peer(i))))
    weight = dot(member[...], wa[...], ((1,), (1,)), exact)
    sig = 1.0 / (1.0 + jnp.exp(-gate))
    silu = gate * sig
    hidden = silu * upper
    scaled = weight * hidden
    spread(0, [(scaled.T.astype(BF16), wd)])
    across(1)
    reduce_core(0)
    finish(1)
    value = rows_by_tokens(wd, cs)
    d_hidden = weight * value
    d_gate = d_hidden * upper * (sig * (1.0 + gate * (1.0 - sig)))
    d_up = d_hidden * silu
    factors = jnp.concatenate([scaled.astype(BF16), d_gate.astype(BF16), d_up.astype(BF16), label[...]], 1)
    fs[...] = dot(pack[...], factors, ((1,), (0,))).astype(BF16)
    each(0, n_ep - 1, lambda i: f_send(i).start())
    spread(1, [(d_gate.T.astype(BF16), wg), (d_up.T.astype(BF16), wu)])
    reduce_y(0)
    sw[...] = dot((hidden * value).T, member[...], ((1,), (0,)), exact)
    each(0, n_ep - 1, lambda i: s_send(i).start())
    rw[p] = sw[rows_at(here, rows)]
    reduce_core(1)
    reduce_x(0)
    fr[rows_at(p, PACK)] = fs[rows_at(p, PACK)]
    each(0, n_ep - 1, lambda i: got(fr.at[rows_at(ep_peer(i), PACK)], r_f.at[ep_peer(i)], (t, ep_peer(i))))
    slots = grads.shape[1]
    slot_ids = lax.broadcasted_iota(jnp.int32, (n_ep * PACK, LANES), 1).astype(F32) + 1.0
    chosen = jnp.where(fr[:, 3 * count :].astype(F32) == slot_ids, 1.0, 0.0)
    placing = chosen.T.astype(BF16)[:slots]
    placed = dot(placing, fr[:, : 3 * count], ((1,), (0,))).astype(BF16)

    keep = grads.shape[0]
    stores = []
    for index, wide, ref in ((1, xs, grad_gate), (2, xs, grad_up), (0, cs, grad_down)):
        slot = len(stores) % keep
        if len(stores) >= keep:
            stores[len(stores) - keep].wait()
        factor = placed[:, index * count : (index + 1) * count]

        def gradient(j):
            span = pl.ds(pl.multiple_of(j * step_cols, LANES), step_cols)
            grads[slot, :, span] = dot(factor, wide[:, span], ((1,), (0,))).astype(BF16)

        each(0, width // step_cols, gradient)
        stores.append(pltpu.make_async_copy(grads.at[slot], ref, s_g.at[len(stores)]))
        stores[-1].start()
    reduce_y(1)
    each(0, n_ep - 1, lambda i: got(rw.at[ep_peer(i)], r_s.at[ep_peer(i)], (t, ep_peer(i))))
    rv[t] = jnp.sum(rw[...], 0)
    each(0, n_tp - 1, lambda i: v_send(i).start())
    reduce_x(1)
    reduce_z(0, out)

    def v_got(i):
        source = lax.rem(t + 1 + i, n_tp)
        got(rv.at[source], r_v.at[source], (source, p))

    each(0, n_tp - 1, v_got)
    dwt[...] = jnp.sum(rv[...], 0)
    reduce_z(1, dtok)
    for store in stores[-keep:]:
        store.wait()
    each(0, n_ep - 1, lambda i: w_send(i).wait_send())
    each(0, n_ep - 1, lambda i: f_send(i).wait_send())
    each(0, n_ep - 1, lambda i: s_send(i).wait_send())
    each(0, n_tp - 1, lambda i: v_send(i).wait_send())
    for a in range(2):
        each(0, n_z - 1, lambda i: z_send(a, i).wait_send())
        each(0, n_z, lambda k: each(0, n_x - 1, lambda i: x_send(a, k, i).wait_send()))
        each(1, n_ep, lambda k: each(0, n_y - 1, lambda i: y_send(a, k, i).wait_send()))
        each(1, n_ep, lambda k: each(0, n_y, lambda q: c_send(a, k, q).wait_send()))
        each(0, n_y, lambda q: each(0, n_x, lambda g: rc_send(a, q, g).wait_send()))
        each(0, n_y - 1, lambda i: each(0, n_x, lambda g: ry_send(a, i, g).wait_send()))
        each(0, n_x - 1, lambda i: rx_send(a, i).wait_send())
        each(0, n_z - 1, lambda i: rz_send(a, i).wait_send())


def earlier_same(labels):
    count = labels.shape[0]
    row_iota = lax.broadcasted_iota(jnp.int32, (count, count), 0)
    col_iota = lax.broadcasted_iota(jnp.int32, (count, count), 1)
    same = (labels[:, None] == labels[None, :]) & (col_iota < row_iota)
    return jnp.sum(same.astype(jnp.int32), 1)


def body(tokens, cotangent, w_gate, w_up, w_down, neuron_expert, neuron_slot, choice_expert, choice_weight):
    n_ep, n_tp = lax.axis_size("ep"), lax.axis_size("tp")
    n_y, n_z, n_x = grid_of(n_tp, n_ep)
    neurons, width = w_gate.shape
    rows = tokens.shape[0]
    count = n_ep * rows
    quarter = width // n_tp
    group = n_z * rows
    peer_slots = 2 * ((neurons + n_ep - 1) // n_ep)
    capacity = n_ep * peer_slots // E_DEV
    slots = E_DEV * capacity
    assert peer_slots <= PACK and slots <= LANES and E_DEV * n_ep <= LANES

    ids = jnp.arange(LANES, dtype=jnp.int32)
    named = choice_expert[:, :, None] == ids[None, None, :]
    by_expert = jnp.sum(jnp.where(named, choice_weight[:, :, None], 0.0), 1)
    member = (neuron_expert[:, None] == ids[None, :]).astype(F32)
    owner = neuron_expert // E_DEV
    target = owner * PACK + earlier_same(owner)
    pack = (jnp.arange(n_ep * PACK, dtype=jnp.int32)[:, None] == target[None, :]).astype(BF16)
    label = (neuron_expert % E_DEV * capacity + neuron_slot + 1).astype(F32).astype(BF16)
    label = jnp.broadcast_to(label[:, None], (neurons, LANES))

    keep = 3 if count <= 2 * LANES else 2
    vmem = pl.BlockSpec(memory_space=pltpu.VMEM)
    anywhere = pl.BlockSpec(memory_space=pl.ANY)
    dma = pltpu.SemaphoreType.DMA
    small = jax.ShapeDtypeStruct((rows, quarter), BF16)
    grad = jax.ShapeDtypeStruct((slots, width), BF16)
    output, d_tokens, per_expert, d_gate, d_up, d_down = pl.pallas_call(
        functools.partial(kernel, n_tp, n_ep),
        out_shape=(small, small, jax.ShapeDtypeStruct((rows, LANES), F32), grad, grad, grad),
        in_specs=[vmem] * 9,
        out_specs=[vmem] * 3 + [anywhere] * 3,
        scratch_shapes=[
            pltpu.VMEM((count, width), BF16),
            pltpu.VMEM((count, width), BF16),
            pltpu.VMEM((count, LANES), F32),
            pltpu.VMEM((n_ep * PACK, 3 * count + LANES), BF16),
            pltpu.VMEM((n_ep * PACK, 3 * count + LANES), BF16),
            pltpu.VMEM((count, LANES), F32),
            pltpu.VMEM((n_ep, rows, LANES), F32),
            pltpu.VMEM((n_tp, rows, LANES), F32),
            pltpu.VMEM((2, n_tp, count, quarter), BF16),
            pltpu.VMEM((2, n_y, n_x, group, quarter), BF16),
            pltpu.VMEM((2, n_y - 1, n_x, group, quarter), BF16),
            pltpu.VMEM((2, n_x, group, quarter), BF16),
            pltpu.VMEM((2, n_z, rows, quarter), BF16),
            pltpu.VMEM((keep, slots, width), BF16),
            dma((2, n_z)),
            dma((2, n_z, n_x)),
            dma((2, n_ep, n_y)),
            dma((2, n_ep, n_y)),
            dma((2, n_ep, n_tp)),
            dma((n_ep,)),
            dma((n_ep,)),
            dma((n_ep,)),
            dma((n_ep,)),
            dma((n_ep,)),
            dma((n_ep,)),
            dma((n_tp,)),
            dma((n_tp,)),
            dma((2, n_y, n_x)),
            dma((2, n_y, n_x)),
            dma((2, n_y, n_x)),
            dma((2, n_y, n_x)),
            dma((2, n_x)),
            dma((2, n_x)),
            dma((2, n_z)),
            dma((2, n_z)),
            dma((3,)),
        ],
        compiler_params=pltpu.CompilerParams(
            collective_id=0, has_side_effects=True, vmem_limit_bytes=62 * 1024 * 1024
        ),
    )(tokens, cotangent, w_gate, w_up, w_down, by_expert, member, pack, label)
    d_weight = jnp.sum(jnp.where(named, per_expert[:, None, :], 0.0), 2)

    def expert_blocks(rows_):
        return rows_.reshape(E_DEV, capacity, width)

    return output, d_tokens, d_weight, expert_blocks(d_gate), expert_blocks(d_up), expert_blocks(d_down)


def solution(mesh):
    in_specs = (
        P("ep", None),
        P("ep", None),
        P(("tp", "ep"), None),
        P(("tp", "ep"), None),
        P(("tp", "ep"), None),
        P(("tp", "ep")),
        P(("tp", "ep")),
        P("ep", None),
        P("ep", None),
    )
    out_specs = (
        P("ep", "tp"),
        P("ep", "tp"),
        P("ep", None),
        P("ep", "tp", None),
        P("ep", "tp", None),
        P("ep", "tp", None),
    )
    return jax.shard_map(body, mesh=mesh, in_specs=in_specs, out_specs=out_specs, check_vma=False)
```

time: 392 us -> 95.6 us (0.24)
  waiting for transfers between devices: 240 us -> 0 us
  blocking collectives: 113 us -> 0 us
  Pallas kernels: 0 us -> 77.9 us
  matrix products: 18.2 us -> 0 us
  between operations: 14.9 us -> 0.66 us
  local copies, waits for them, and re-layouts: 4.12 us -> 12.2 us
    reduce_scatter x4 -> x0, waiting for transfers between devices: 143 us -> none  [the longest x2 116 us: to_owner(): return lax.psum_scatter(part, 'ep', scatter_dimension=0, tiled=True)]
    all_gather x2 -> x0, waiting for transfers between devices: 94.8 us -> none  [the longest x1 48.6 us: body(): x_all = lax.all_gather(tokens, 'ep', axis=0, tiled=True)]
    pallas_call x0 -> x1, Pallas kernels: none -> 77.9 us  [body(): pl.pallas_call(functools.partial(kernel, n_tp, n_ep), out_shape=(small, s...]
    all_gather x2 -> x0, blocking collectives: 61.5 us -> none  [the longest x1 31 us: body(): factors_all = lax.all_gather(factors, 'ep', axis=0, tiled=True)]
    psum x1 -> x0, blocking collectives: 39.6 us -> none  [body(): per_expert = lax.psum(per_expert, ('tp', 'ep'))]
    dot_general x11 -> x0, matrix products: 18.2 us -> none  [the longest x3 6.1 us: from_neurons(): return jnp.einsum('nt,nd->td', factor, rows, preferred_element_type=f32)]
    unnamed x1 -> x0, blocking collectives: 11.4 us -> none
    unnamed x17 -> x12, local copies, waits for them, and re-layouts: 3.45 us -> 11.5 us
  transfers between devices with their start and end apart: 6 -> 0, of which waited for: 5 -> 0; matrix products, arithmetic and copies ran while one was open for 5% -> 0% of each run, Pallas kernels for 0% -> 0%
where the time goes in v2:
time: 95.6 us; the launch traced here: 95.2 us
  Pallas kernels  77.9 us (81%)
  local copies, waits for them, and re-layouts  12.2 us (13%)
  other arithmetic  4.39 us (5%)
    pallas_call x1, Pallas kernels, body(): pl.pallas_call(functools.partial(kernel, n_tp, n_ep), out_shape=(small, s...  77.9 us
    unnamed x12, local copies, waits for them, and re-layouts  11.5 us

profile of v2, /device:TPU:0, one launch (start us, length us, event | category | flops | bytes accessed | tf_op | source)
XLA Modules:
  0.0 95.2 jit_solution(2993726859568168098)
XLA Ops:
  0.6 0.7 convert_convert_fusion
  1.3 0.2 convert_reduce_fusion
  1.5 0.8 copy.17
  2.3 0.8 copy.18
  3.0 0.7 select_reduce_fusion.1.we
  3.7 0.7 broadcast_in_dim.22.label
  4.4 1.3 %fusion.1.member = f32[56,128]{1,0:T(8,128)} fusion(s32[56]{0:T(128)} %param.14), kind=kLoop, calls=%fused_computation.8 | loop fusion | flops 14336 | bytes 28896 | tf_op jit(solution)/shard_map/convert_element_type | solution.py:391
  5.7 0.6 fusion.pack
  6.4 77.9 %shard_map.136 = (bf16[16,2048]{1,0:T(8,128)(2,1)}, bf16[16,2048]{1,0:T(8,128)(2,1)}, f32[16,128]{1,0:T(8,128)}, bf16[112,8192]{1,0:T(8,128)(2,1)}, bf16[112,819...) custom-call(bf16[16,8192]{1,0:T(8,128)(2,1)} %tok.1, bf16[16,8192]{1,0:T(8,128)(2,1)} %cot.1, bf16[56,8192]{1,0:T(8,128)(2,1)} %wg.1, ...), custom_call_target="tpu_custom_call" | custom-call | tf_op jit(solution)/shard_map/pallas_call | solution.py:404
  84.3 0.9 select_reduce_fusion
  85.2 0.7 copy.19
  85.9 1.5 %copy.25 = bf16[16,2048]{1,0:T(8,128)(2,1)} copy(bf16[16,2048]{1,0:T(8,128)(2,1)} %get-tuple-element.32) | data formatting | bytes 131072
  87.3 1.5 %copy.26 = bf16[16,2048]{1,0:T(8,128)(2,1)} copy(bf16[16,2048]{1,0:T(8,128)(2,1)} %get-tuple-element.33) | data formatting | bytes 131072
  88.8 0.0 copy-start.1
  88.8 3.0 %copy.27 = bf16[2,56,8192]{2,1,0:T(8,128)(2,1)} copy(bf16[2,56,8192]{2,1,0:T(8,128)(2,1)} %bitcast.5) | data formatting | bytes 3670016
  91.8 0.0 copy-done.1
  91.8 0.0 copy-start
  91.8 1.2 %copy.28 = bf16[2,56,8192]{2,1,0:T(8,128)(2,1)} copy(bf16[2,56,8192]{2,1,0:T(8,128)(2,1)S(1)} %bitcast.4) | data formatting | bytes 3670016
  93.0 0.9 copy-done
  94.0 1.2 %copy.29 = bf16[2,56,8192]{2,1,0:T(8,128)(2,1)} copy(bf16[2,56,8192]{2,1,0:T(8,128)(2,1)S(1)} %bitcast.3) | data formatting | bytes 3670016
  (1 shorter events, 0.0 us)
Async XLA Ops:
  88.8 3.0 %copy-start.1 = (bf16[112,8192]{1,0:T(8,128)(2,1)S(1)}, bf16[112,8192]{1,0:T(8,128)(2,1)}, u32[]{:S(2)}) copy-start(bf16[112,8192]{1,0:T(8,128)(2,1)} %get-tuple-element.16) | copy-start | bytes 5505028
  91.8 2.2 %copy-start = (bf16[112,8192]{1,0:T(8,128)(2,1)S(1)}, bf16[112,8192]{1,0:T(8,128)(2,1)}, u32[]{:S(2)}) copy-start(bf16[112,8192]{1,0:T(8,128)(2,1)} %get-tuple-element.17) | copy-start | bytes 5505028

commit v3 on v2

--- a/solution.py
+++ b/solution.py
@@ -38,10 +38,10 @@
 
 
 def kernel(
-    n_tp, n_ep, tok, cot, wg, wu, wd, we, member, pack, label,
+    n_tp, n_ep, tok, cot, wg, wu, wd, ne, ns, ce, cw,
     out, dtok, dwt, grad_gate, grad_up, grad_down,
     xs, cs, wa, fs, fr, sw, rw, rv, part, rc, ry, rx, rz, grads,
-    s_z, s_x, s_y, s_c, r_ag, s_w, r_w, s_f, r_f, s_s, r_s, s_v, r_v,
+    s_z, s_zs, s_x, s_xs, s_y, s_c, s_cs, r_ag, r_sd, s_w, r_w, s_f, r_f, s_s, r_s, s_v, r_v,
     s_rc, r_rc, s_ry, r_ry, s_rx, r_rx, s_rz, r_rz, s_g,
 ):
     n_y, n_z, n_x = grid_of(n_tp, n_ep)
@@ -83,32 +83,69 @@
     def cols_at(q):
         return pl.ds(pl.multiple_of(q * quarter, LANES), quarter)
 
+    side = quarter // 2
+
     def block(a, k, q):
         return bufs[a].at[rows_at(k, rows), cols_at(q)]
 
+    def side_block(a, k, q):
+        return bufs[a].at[rows_at(k, rows), pl.ds(pl.multiple_of(q * quarter, LANES), side)]
+
+    def rest_block(a, k, q):
+        return bufs[a].at[rows_at(k, rows), pl.ds(pl.multiple_of(q * quarter + side, LANES), quarter - side)]
+
     def ranked(k):
         return place(lax.rem(z + n_z - lax.rem(k, n_z), n_z), lax.rem(x + k // n_z, n_x))
+
+    def next_y(i):
+        return lax.rem(y + 1 + i, n_y)
+
+    sibling = (y * CORES + other, p)
 
     def z_send(a, i):
         b = block(a, here, t)
         return copy(b, b, s_z.at[a, i], r_ag.at[a, here, t], at(lax.rem(z + 1 + i, n_z), x))
 
+    def zs_send(a, i, j):
+        q = next_y(j) * CORES + c
+        b = side_block(a, here, q)
+        return copy(b, b, s_zs.at[a, i, j], r_sd.at[a, here, q], at(lax.rem(z + 1 + i, n_z), x))
+
     def x_send(a, k, i):
         b = block(a, ranked(k), t)
         return copy(b, b, s_x.at[a, k, i], r_ag.at[a, ranked(k), t], at(z, lax.rem(x + 1 + i, n_x)))
 
+    def xs_send(a, k, i, j):
+        q = next_y(j) * CORES + c
+        b = side_block(a, ranked(k), q)
+        return copy(b, b, s_xs.at[a, k, i, j], r_sd.at[a, ranked(k), q], at(z, lax.rem(x + 1 + i, n_x)))
+
     def y_send(a, k, i):
+        b = rest_block(a, ranked(k), t)
+        return copy(b, b, s_y.at[a, k, i], r_ag.at[a, ranked(k), t], (next_y(i) * CORES + c, p))
+
+    def c_send(a, k):
         b = block(a, ranked(k), t)
-        to = lax.rem(y + 1 + i, n_y) * CORES + c
-        return copy(b, b, s_y.at[a, k, i], r_ag.at[a, ranked(k), t], (to, p))
-
-    def c_send(a, k, qy):
-        q = qy * CORES + c
-        b = block(a, ranked(k), q)
-        return copy(b, b, s_c.at[a, k, qy], r_ag.at[a, ranked(k), q], (y * CORES + other, p))
+        return copy(b, b, s_c.at[a, k, n_y - 1], r_ag.at[a, ranked(k), t], sibling)
+
+    def cr_send(a, k, i):
+        q = next_y(i) * CORES + c
+        b = rest_block(a, ranked(k), q)
+        return copy(b, b, s_c.at[a, k, i], r_ag.at[a, ranked(k), q], sibling)
+
+    def cs_send(a, k, i):
+        q = next_y(i) * CORES + c
+        b = side_block(a, ranked(k), q)
+        return copy(b, b, s_cs.at[a, k, i], r_sd.at[a, ranked(k), q], sibling)
 
     def arrived(a, k, q):
-        got(block(a, ranked(k), q), r_ag.at[a, ranked(k), q], (y * CORES + other, p))
+        got(block(a, ranked(k), q), r_ag.at[a, ranked(k), q], sibling)
+
+    def side_arrived(a, k, q):
+        got(side_block(a, ranked(k), q), r_sd.at[a, ranked(k), q], sibling)
+
+    def rest_arrived(a, k, q):
+        got(rest_block(a, ranked(k), q), r_ag.at[a, ranked(k), q], sibling)
 
     def w_send(i):
         b = wa.at[rows_at(here, rows)]
@@ -153,49 +190,86 @@
     )
     xs[rows_at(here, rows)] = tok[...]
     cs[rows_at(here, rows)] = cot[...]
-    wa[rows_at(here, rows)] = we[...]
     pl.semaphore_wait(barrier, n_ep - 1 + n_tp - 1)
 
     for a in range(2):
         each(0, n_z - 1, lambda i: z_send(a, i).start())
         each(0, n_x - 1, lambda i: x_send(a, 0, i).start())
+        each(0, n_z - 1, lambda i: each(0, n_y - 1, lambda j: zs_send(a, i, j).start()))
+        each(0, n_x - 1, lambda i: each(0, n_y - 1, lambda j: xs_send(a, 0, i, j).start()))
+
+    experts = lax.broadcasted_iota(jnp.int32, (rows, LANES), 1)
+    by_expert = jnp.zeros((rows, LANES), F32)
+    for k in range(ce.shape[1]):
+        by_expert = by_expert + jnp.where(ce[:, k : k + 1] == experts, cw[:, k : k + 1], 0.0)
+    wa[rows_at(here, rows)] = by_expert
     each(0, n_ep - 1, lambda i: w_send(i).start())
 
-    def forward(a):
-        def near(k):
-            arrived(a, k, t)
+    neurons = wg.shape[0]
+    slots = grads.shape[1]
+    named = ne[...]
+    owner = lax.div(named, E_DEV)
+
+    def ids(size):
+        return lax.broadcasted_iota(jnp.int32, (size, neurons), 0)
+
+    def ones(mask):
+        return jnp.where(mask, 1.0, 0.0)
+
+    member = ones(ids(LANES) == named).T
+    owned = ones(ids(n_ep) == owner)
+    order = ones(ids(neurons) < lax.broadcasted_iota(jnp.int32, (neurons, neurons), 1))
+    before = dot(owned.astype(BF16), order.astype(BF16), ((1,), (0,)))
+    target = owner.astype(F32) * PACK + jnp.sum(owned * before, 0, keepdims=True)
+    pack = ones(ids(n_ep * PACK).astype(F32) == target).astype(BF16)
+    label = (lax.rem(named, E_DEV) * (slots // E_DEV) + ns[...] + 1).astype(F32)
+    label = jnp.broadcast_to(label, (LANES, neurons)).T.astype(BF16)
+
+    def forward(a, k, near):
+        arrived(a, k, t)
+        if near:
             each(0, n_x - 1, lambda i: x_send(a, k, i).start())
-            each(0, n_y - 1, lambda i: y_send(a, k, i).start())
-            c_send(a, k, y).start()
-
-        def far(k):
-            arrived(a, k, t)
-            each(0, n_y - 1, lambda i: y_send(a, k, i).start())
-            c_send(a, k, y).start()
-
-        each(1, n_z, near)
-        each(n_z, n_ep, far)
-
-    def across(a):
-        def from_y(i):
-            qy = lax.rem(y + 1 + i, n_y)
+        each(0, n_y - 1, lambda i: y_send(a, k, i).start())
+        c_send(a, k).start()
+
+        def one(j):
+            side_arrived(a, k, next_y(j) * CORES + c)
+            if near:
+                each(0, n_x - 1, lambda i: xs_send(a, k, i, j).start())
+            cs_send(a, k, j).start()
+
+        each(0, n_y - 1, one)
+
+    def across(a, k):
+        def one(i):
+            rest_arrived(a, k, next_y(i) * CORES + c)
+            cr_send(a, k, i).start()
+
+        each(0, n_y - 1, one)
+
+    def project(a, weights):
+        def add(q, totals):
+            wide = bufs[a][:, cols_at(q)]
+            return tuple(total + dot(weight[:, cols_at(q)], wide, ((1,), (1,))) for total, weight in zip(totals, weights))
+
+        def mine(i, totals):
+            return add(lax.rem(y + i, n_y) * CORES + c, totals)
+
+        def theirs(i, totals):
+            q = next_y(i) * CORES + other
 
             def one(k):
-                arrived(a, k, qy * CORES + c)
-                c_send(a, k, qy).start()
+                rest_arrived(a, k, q)
+                side_arrived(a, k, q)
 
             each(1, n_ep, one)
-
-        each(0, n_y - 1, from_y)
-
-    def finish(a):
-        each(0, n_y, lambda qy: each(1, n_ep, lambda k: arrived(a, k, qy * CORES + other)))
-
-    def rows_by_tokens(weight, wide):
-        def step(q, total):
-            return total + dot(weight[:, cols_at(q)], wide[:, cols_at(q)], ((1,), (1,)))
-
-        return lax.fori_loop(0, n_tp, step, jnp.zeros((weight.shape[0], count), F32))
+            return add(q, totals)
+
+        totals = tuple(jnp.zeros((neurons, count), F32) for _ in weights)
+        totals = lax.fori_loop(0, n_y, mine, totals)
+        each(1, n_ep, lambda k: arrived(a, k, y * CORES + other))
+        totals = add(y * CORES + other, totals)
+        return lax.fori_loop(0, n_y - 1, theirs, totals)
 
     step_cols = min(quarter, 512)
 
@@ -280,39 +354,41 @@
         result[...] = total.astype(BF16)
 
     exact = lax.Precision.HIGHEST
-    forward(0)
-    forward(1)
-    across(0)
-    finish(0)
-    gate = rows_by_tokens(wg, xs)
-    upper = rows_by_tokens(wu, xs)
+    each(1, n_z, lambda k: forward(0, k, True))
+    each(n_z, n_ep, lambda k: forward(0, k, False))
+
+    def both(k, near):
+        across(0, k)
+        forward(1, k, near)
+
+    each(1, n_z, lambda k: both(k, True))
+    each(n_z, n_ep, lambda k: both(k, False))
+    gate, upper = project(0, (wg, wu))
     each(0, n_ep - 1, lambda i: got(wa.at[rows_at(place_of(ep_peer(i)), rows)], r_w.at[place_of(ep_peer(i))], (t, ep_peer(i))))
-    weight = dot(member[...], wa[...], ((1,), (1,)), exact)
+    weight = dot(member, wa[...], ((1,), (1,)), exact)
     sig = 1.0 / (1.0 + jnp.exp(-gate))
     silu = gate * sig
     hidden = silu * upper
     scaled = weight * hidden
     spread(0, [(scaled.T.astype(BF16), wd)])
-    across(1)
+    each(1, n_ep, lambda k: across(1, k))
     reduce_core(0)
-    finish(1)
-    value = rows_by_tokens(wd, cs)
+    (value,) = project(1, (wd,))
     d_hidden = weight * value
     d_gate = d_hidden * upper * (sig * (1.0 + gate * (1.0 - sig)))
     d_up = d_hidden * silu
-    factors = jnp.concatenate([scaled.astype(BF16), d_gate.astype(BF16), d_up.astype(BF16), label[...]], 1)
-    fs[...] = dot(pack[...], factors, ((1,), (0,))).astype(BF16)
+    factors = jnp.concatenate([scaled.astype(BF16), d_gate.astype(BF16), d_up.astype(BF16), label], 1)
+    fs[...] = dot(pack, factors, ((1,), (0,))).astype(BF16)
     each(0, n_ep - 1, lambda i: f_send(i).start())
     spread(1, [(d_gate.T.astype(BF16), wg), (d_up.T.astype(BF16), wu)])
     reduce_y(0)
-    sw[...] = dot((hidden * value).T, member[...], ((1,), (0,)), exact)
+    sw[...] = dot((hidden * value).T, member, ((1,), (0,)), exact)
     each(0, n_ep - 1, lambda i: s_send(i).start())
     rw[p] = sw[rows_at(here, rows)]
     reduce_core(1)
     reduce_x(0)
     fr[rows_at(p, PACK)] = fs[rows_at(p, PACK)]
     each(0, n_ep - 1, lambda i: got(fr.at[rows_at(ep_peer(i), PACK)], r_f.at[ep_peer(i)], (t, ep_peer(i))))
-    slots = grads.shape[1]
     slot_ids = lax.broadcasted_iota(jnp.int32, (n_ep * PACK, LANES), 1).astype(F32) + 1.0
     chosen = jnp.where(fr[:, 3 * count :].astype(F32) == slot_ids, 1.0, 0.0)
     placing = chosen.T.astype(BF16)[:slots]
@@ -345,7 +421,13 @@
         got(rv.at[source], r_v.at[source], (source, p))
 
     each(0, n_tp - 1, v_got)
-    dwt[...] = jnp.sum(rv[...], 0)
+    per_expert = jnp.sum(rv[...], 0)
+    choice = lax.broadcasted_iota(jnp.int32, dwt.shape, 1)
+    picked = jnp.zeros(dwt.shape, F32)
+    for k in range(ce.shape[1]):
+        value_k = jnp.sum(jnp.where(ce[:, k : k + 1] == experts, per_expert, 0.0), 1, keepdims=True)
+        picked = picked + jnp.where(choice == k, value_k, 0.0)
+    dwt[...] = picked
     reduce_z(1, dtok)
     for store in stores[-keep:]:
         store.wait()
@@ -355,21 +437,46 @@
     each(0, n_tp - 1, lambda i: v_send(i).wait_send())
     for a in range(2):
         each(0, n_z - 1, lambda i: z_send(a, i).wait_send())
-        each(0, n_z, lambda k: each(0, n_x - 1, lambda i: x_send(a, k, i).wait_send()))
-        each(1, n_ep, lambda k: each(0, n_y - 1, lambda i: y_send(a, k, i).wait_send()))
-        each(1, n_ep, lambda k: each(0, n_y, lambda q: c_send(a, k, q).wait_send()))
+        each(0, n_z - 1, lambda i: each(0, n_y - 1, lambda j: zs_send(a, i, j).wait_send()))
+
+        def row_sent(k):
+            def one(i):
+                x_send(a, k, i).wait_send()
+                each(0, n_y - 1, lambda j: xs_send(a, k, i, j).wait_send())
+
+            each(0, n_x - 1, one)
+
+        def block_sent(k):
+            def one(i):
+                y_send(a, k, i).wait_send()
+                cr_send(a, k, i).wait_send()
+                cs_send(a, k, i).wait_send()
+
+            c_send(a, k).wait_send()
+            each(0, n_y - 1, one)
+
+        each(0, n_z, row_sent)
+        each(1, n_ep, block_sent)
         each(0, n_y, lambda q: each(0, n_x, lambda g: rc_send(a, q, g).wait_send()))
         each(0, n_y - 1, lambda i: each(0, n_x, lambda g: ry_send(a, i, g).wait_send()))
         each(0, n_x - 1, lambda i: rx_send(a, i).wait_send())
         each(0, n_z - 1, lambda i: rz_send(a, i).wait_send())
 
 
-def earlier_same(labels):
-    count = labels.shape[0]
-    row_iota = lax.broadcasted_iota(jnp.int32, (count, count), 0)
-    col_iota = lax.broadcasted_iota(jnp.int32, (count, count), 1)
-    same = (labels[:, None] == labels[None, :]) & (col_iota < row_iota)
-    return jnp.sum(same.astype(jnp.int32), 1)
+def hand_on(*refs):
+    arrays, sems = refs[:-1], refs[-1]
+    half = len(arrays) // 2
+    small, large = slice(0, 3), slice(3, half)
+    stores = [
+        pltpu.make_async_copy(src, dst, sems.at[i])
+        for i, (src, dst) in enumerate(zip(arrays[:half][large], arrays[half:][large]))
+    ]
+    for store in stores:
+        store.start()
+    for src, dst in zip(arrays[:half][small], arrays[half:][small]):
+        dst[...] = src[...]
+    for store in stores:
+        store.wait()
 
 
 def body(tokens, cotangent, w_gate, w_up, w_down, neuron_expert, neuron_slot, choice_expert, choice_weight):
@@ -385,25 +492,16 @@
     slots = E_DEV * capacity
     assert peer_slots <= PACK and slots <= LANES and E_DEV * n_ep <= LANES
 
-    ids = jnp.arange(LANES, dtype=jnp.int32)
-    named = choice_expert[:, :, None] == ids[None, None, :]
-    by_expert = jnp.sum(jnp.where(named, choice_weight[:, :, None], 0.0), 1)
-    member = (neuron_expert[:, None] == ids[None, :]).astype(F32)
-    owner = neuron_expert // E_DEV
-    target = owner * PACK + earlier_same(owner)
-    pack = (jnp.arange(n_ep * PACK, dtype=jnp.int32)[:, None] == target[None, :]).astype(BF16)
-    label = (neuron_expert % E_DEV * capacity + neuron_slot + 1).astype(F32).astype(BF16)
-    label = jnp.broadcast_to(label[:, None], (neurons, LANES))
-
     keep = 3 if count <= 2 * LANES else 2
     vmem = pl.BlockSpec(memory_space=pltpu.VMEM)
     anywhere = pl.BlockSpec(memory_space=pl.ANY)
     dma = pltpu.SemaphoreType.DMA
     small = jax.ShapeDtypeStruct((rows, quarter), BF16)
     grad = jax.ShapeDtypeStruct((slots, width), BF16)
-    output, d_tokens, per_expert, d_gate, d_up, d_down = pl.pallas_call(
+    shapes = (small, small, jax.ShapeDtypeStruct(choice_weight.shape, F32), grad, grad, grad)
+    results = pl.pallas_call(
         functools.partial(kernel, n_tp, n_ep),
-        out_shape=(small, small, jax.ShapeDtypeStruct((rows, LANES), F32), grad, grad, grad),
+        out_shape=shapes,
         in_specs=[vmem] * 9,
         out_specs=[vmem] * 3 + [anywhere] * 3,
         scratch_shapes=[
@@ -422,9 +520,13 @@
             pltpu.VMEM((2, n_z, rows, quarter), BF16),
             pltpu.VMEM((keep, slots, width), BF16),
             dma((2, n_z)),
+            dma((2, n_z, n_y)),
             dma((2, n_z, n_x)),
+            dma((2, n_z, n_x, n_y)),
             dma((2, n_ep, n_y)),
             dma((2, n_ep, n_y)),
+            dma((2, n_ep, n_y)),
+            dma((2, n_ep, n_tp)),
             dma((2, n_ep, n_tp)),
             dma((n_ep,)),
             dma((n_ep,)),
@@ -447,8 +549,17 @@
         compiler_params=pltpu.CompilerParams(
             collective_id=0, has_side_effects=True, vmem_limit_bytes=62 * 1024 * 1024
         ),
-    )(tokens, cotangent, w_gate, w_up, w_down, by_expert, member, pack, label)
-    d_weight = jnp.sum(jnp.where(named, per_expert[:, None, :], 0.0), 2)
+    )(
+        tokens, cotangent, w_gate, w_up, w_down,
+        neuron_expert.reshape(1, -1), neuron_slot.reshape(1, -1), choice_expert, choice_weight,
+    )
+    output, d_tokens, d_weight, d_gate, d_up, d_down = pl.pallas_call(
+        hand_on,
+        out_shape=shapes,
+        in_specs=[vmem] * 3 + [anywhere] * 3,
+        out_specs=[vmem] * 3 + [anywhere] * 3,
+        scratch_shapes=[dma((3,))],
+    )(*results)
 
     def expert_blocks(rows_):
         return rows_.reshape(E_DEV, capacity, width)

time: 95.6 us -> 252 us (2.64)
  Pallas kernels: 77.9 us -> 247 us
  local copies, waits for them, and re-layouts: 12.2 us -> 4.07 us
  other arithmetic: 4.39 us -> 0 us
    pallas_call x1 -> x2, Pallas kernels: 77.9 us -> 247 us  [the longest x1 169 us: body(): pl.pallas_call(hand_on, out_shape=shapes, in_specs=[vmem] * 3 + [anywhere...]
    unnamed x12 -> x3, local copies, waits for them, and re-layouts: 11.5 us -> 4.07 us
    convert_element_type x3 -> x0, other arithmetic: 2.65 us -> none  [the longest x1 1.34 us: body(): member = (neuron_expert[:, None] == ids[None, :]).astype(F32)]
where the time goes in v3:
time: 252 us
  Pallas kernels  247 us (98%)
  local copies, waits for them, and re-layouts  4.07 us (2%)
    pallas_call x1, Pallas kernels, body(): pl.pallas_call(hand_on, out_shape=shapes, in_specs=[vmem] * 3 + [anywhere...  169 us
    pallas_call x1, Pallas kernels, body(): pl.pallas_call(functools.partial(kernel, n_tp, n_ep), out_shape=shapes, i...  77.8 us

profile of v3, /device:TPU:0, one launch (start us, length us, event | category | flops | bytes accessed | tf_op | source)
XLA Modules:
  0.0 251.9 jit_solution(151871233896051543)
XLA Ops:
  0.6 1.4 copy.15.ce
  2.0 1.4 copy.16.cw
  3.3 77.8 %shard_map.136 = (bf16[16,2048]{1,0:T(8,128)(2,1)}, bf16[16,2048]{1,0:T(8,128)(2,1)}, f32[16,8]{1,0:T(8,128)}, bf16[112,8192]{1,0:T(8,128)(2,1)}, bf16[112,8192]{1,0:T(8,128)(2,1)}, /*index=5*/bf16[112,8192]{1,0:T(8,128)(2,1)}) custom-call(bf16[16,8192]{1,0:T(8,128)(2,1)} %tok.1, bf16[16,8192]{1,0:T(8,128)(2,1)} %cot.1, bf16[56,8192]{1,0:T(8,128)(2,1)} %wg.1, ...), custom_call_target="tpu_custom_call" | custom-call | tf_op jit(solution)/shard_map/pallas_call | solution.py:502
  81.2 169.4 %shard_map.137 = (bf16[16,2048]{1,0:T(8,128)(2,1)}, bf16[16,2048]{1,0:T(8,128)(2,1)}, f32[16,8]{1,0:T(8,128)}, bf16[112,8192]{1,0:T(8,128)(2,1)}, bf16[112,8192]{1,0:T(8,128)(2,1)}, /*index=5*/bf16[112,8192]{1,0:T(8,128)(2,1)}) custom-call(bf16[16,2048]{1,0:T(8,128)(2,1)} %get-tuple-element.18.refs_0_, bf16[16,2048]{1,0:T(8,128)(2,1)} %get-tuple-element.19.refs_1_, ...), custom_call_target="tpu_custom_call" | custom-call | tf_op jit(solution)/shard_map/pallas_call | solution.py:556
  250.6 1.4 copy.17

commit v4 on v3

--- a/solution.py
+++ b/solution.py
@@ -39,9 +39,9 @@
 
 def kernel(
     n_tp, n_ep, tok, cot, wg, wu, wd, ne, ns, ce, cw,
-    out, dtok, dwt, grad_gate, grad_up, grad_down,
-    xs, cs, wa, fs, fr, sw, rw, rv, part, rc, ry, rx, rz, grads,
-    s_z, s_zs, s_x, s_xs, s_y, s_c, s_cs, r_ag, r_sd, s_w, r_w, s_f, r_f, s_s, r_s, s_v, r_v,
+    out, dtok, dwt, placed, x_out, c_out,
+    xs, cs, wa, fs, fr, sw, rw, rv, part, rc, ry, rx, rz,
+    s_z, s_x, s_y, s_c, r_ag, r_sd, r_c, s_w, r_w, s_f, r_f, s_s, r_s, s_v, r_v,
     s_rc, r_rc, s_ry, r_ry, s_rx, r_rx, s_rz, r_rz, s_g,
 ):
     n_y, n_z, n_x = grid_of(n_tp, n_ep)
@@ -73,7 +73,10 @@
         )
 
     def got(dst, recv, device):
-        copy(dst, dst, s_v.at[0], recv, device).wait_recv()
+        copy(dst, dst, s_v, recv, device).wait_recv()
+
+    def taken(ref, sem):
+        pltpu.make_async_copy(ref, ref, sem).wait()
 
     here = place(z, x)
 
@@ -104,39 +107,29 @@
 
     def z_send(a, i):
         b = block(a, here, t)
-        return copy(b, b, s_z.at[a, i], r_ag.at[a, here, t], at(lax.rem(z + 1 + i, n_z), x))
+        return copy(b, b, s_z.at[a], r_ag.at[a, here, t], at(lax.rem(z + 1 + i, n_z), x))
 
     def zs_send(a, i, j):
         q = next_y(j) * CORES + c
         b = side_block(a, here, q)
-        return copy(b, b, s_zs.at[a, i, j], r_sd.at[a, here, q], at(lax.rem(z + 1 + i, n_z), x))
+        return copy(b, b, s_z.at[a], r_sd.at[a, here, q], at(lax.rem(z + 1 + i, n_z), x))
 
     def x_send(a, k, i):
         b = block(a, ranked(k), t)
-        return copy(b, b, s_x.at[a, k, i], r_ag.at[a, ranked(k), t], at(z, lax.rem(x + 1 + i, n_x)))
+        return copy(b, b, s_x.at[a], r_ag.at[a, ranked(k), t], at(z, lax.rem(x + 1 + i, n_x)))
 
     def xs_send(a, k, i, j):
         q = next_y(j) * CORES + c
         b = side_block(a, ranked(k), q)
-        return copy(b, b, s_xs.at[a, k, i, j], r_sd.at[a, ranked(k), q], at(z, lax.rem(x + 1 + i, n_x)))
+        return copy(b, b, s_x.at[a], r_sd.at[a, ranked(k), q], at(z, lax.rem(x + 1 + i, n_x)))
 
     def y_send(a, k, i):
         b = rest_block(a, ranked(k), t)
-        return copy(b, b, s_y.at[a, k, i], r_ag.at[a, ranked(k), t], (next_y(i) * CORES + c, p))
-
-    def c_send(a, k):
-        b = block(a, ranked(k), t)
-        return copy(b, b, s_c.at[a, k, n_y - 1], r_ag.at[a, ranked(k), t], sibling)
-
-    def cr_send(a, k, i):
-        q = next_y(i) * CORES + c
-        b = rest_block(a, ranked(k), q)
-        return copy(b, b, s_c.at[a, k, i], r_ag.at[a, ranked(k), q], sibling)
-
-    def cs_send(a, k, i):
-        q = next_y(i) * CORES + c
-        b = side_block(a, ranked(k), q)
-        return copy(b, b, s_cs.at[a, k, i], r_sd.at[a, ranked(k), q], sibling)
+        return copy(b, b, s_y.at[a], r_ag.at[a, ranked(k), t], (next_y(i) * CORES + c, p))
+
+    def c_send(a, k, qy):
+        b = block(a, ranked(k), qy * CORES + c)
+        return copy(b, b, s_c.at[a], r_c.at[a], sibling)
 
     def arrived(a, k, q):
         got(block(a, ranked(k), q), r_ag.at[a, ranked(k), q], sibling)
@@ -149,38 +142,38 @@
 
     def w_send(i):
         b = wa.at[rows_at(here, rows)]
-        return copy(b, b, s_w.at[i], r_w.at[here], (t, ep_peer(i)))
+        return copy(b, b, s_w, r_w, (t, ep_peer(i)))
 
     def f_send(i):
         to = ep_peer(i)
-        return copy(fs.at[rows_at(to, PACK)], fr.at[rows_at(p, PACK)], s_f.at[i], r_f.at[p], (t, to))
+        return copy(fs.at[rows_at(to, PACK)], fr.at[rows_at(p, PACK)], s_f, r_f, (t, to))
 
     def s_send(i):
         to = ep_peer(i)
-        return copy(sw.at[rows_at(place_of(to), rows)], rw.at[p], s_s.at[i], r_s.at[p], (t, to))
+        return copy(sw.at[rows_at(place_of(to), rows)], rw.at[p], s_s, r_s, (t, to))
 
     def v_send(i):
         to = lax.rem(t + 1 + i, n_tp)
-        return copy(rv.at[t], rv.at[t], s_v.at[i], r_v.at[t], (to, p))
+        return copy(rv.at[t], rv.at[t], s_v, r_v, (to, p))
 
     def rc_send(a, qy, g):
         src = part.at[a, qy * CORES + other, rows_at(g, group)]
-        return copy(src, rc.at[a, qy, g], s_rc.at[a, qy, g], r_rc.at[a, qy, g], (y * CORES + other, p))
+        return copy(src, rc.at[a, qy, g], s_rc.at[a], r_rc.at[a, qy, g], (y * CORES + other, p))
 
     def ry_send(a, i, g):
         to = lax.rem(y + 1 + i, n_y) * CORES + c
         src = part.at[a, to, rows_at(g, group)]
-        return copy(src, ry.at[a, n_y - 2 - i, g], s_ry.at[a, i, g], r_ry.at[a, n_y - 2 - i, g], (to, p))
+        return copy(src, ry.at[a, n_y - 2 - i, g], s_ry.at[a], r_ry.at[a, n_y - 2 - i, g], (to, p))
 
     def rx_send(a, i):
         to = lax.rem(x + 1 + i, n_x)
         src = part.at[a, t, rows_at(to, group)]
-        return copy(src, rx.at[a, x], s_rx.at[a, i], r_rx.at[a, x], at(z, to))
+        return copy(src, rx.at[a, x], s_rx.at[a], r_rx.at[a, x], at(z, to))
 
     def rz_send(a, i):
         to = lax.rem(z + 1 + i, n_z)
         src = part.at[a, t, rows_at(place(to, x), rows)]
-        return copy(src, rz.at[a, z], s_rz.at[a, i], r_rz.at[a, z], at(to, x))
+        return copy(src, rz.at[a, z], s_rz.at[a], r_rz.at[a, z], at(to, x))
 
     barrier = pltpu.get_barrier_semaphore()
     each(0, n_ep - 1, lambda i: pl.semaphore_signal(barrier, inc=1, device_id=(t, ep_peer(i)), device_id_type=MESH))
@@ -198,15 +191,17 @@
         each(0, n_z - 1, lambda i: each(0, n_y - 1, lambda j: zs_send(a, i, j).start()))
         each(0, n_x - 1, lambda i: each(0, n_y - 1, lambda j: xs_send(a, 0, i, j).start()))
 
-    experts = lax.broadcasted_iota(jnp.int32, (rows, LANES), 1)
+    experts = lax.broadcasted_iota(jnp.int32, (rows, LANES), 1).astype(F32)
     by_expert = jnp.zeros((rows, LANES), F32)
-    for k in range(ce.shape[1]):
-        by_expert = by_expert + jnp.where(ce[:, k : k + 1] == experts, cw[:, k : k + 1], 0.0)
+    chosen_by, weight_by = ce[...].astype(F32).T, cw[...].T
+    top = ce.shape[0]
+    for k in range(top):
+        by_expert = by_expert + jnp.where(chosen_by[:, k : k + 1] == experts, weight_by[:, k : k + 1], 0.0)
     wa[rows_at(here, rows)] = by_expert
     each(0, n_ep - 1, lambda i: w_send(i).start())
 
     neurons = wg.shape[0]
-    slots = grads.shape[1]
+    slots = placed.shape[0]
     named = ne[...]
     owner = lax.div(named, E_DEV)
 
@@ -230,20 +225,19 @@
         if near:
             each(0, n_x - 1, lambda i: x_send(a, k, i).start())
         each(0, n_y - 1, lambda i: y_send(a, k, i).start())
-        c_send(a, k).start()
+        c_send(a, k, y).start()
 
         def one(j):
             side_arrived(a, k, next_y(j) * CORES + c)
             if near:
                 each(0, n_x - 1, lambda i: xs_send(a, k, i, j).start())
-            cs_send(a, k, j).start()
 
         each(0, n_y - 1, one)
 
     def across(a, k):
         def one(i):
             rest_arrived(a, k, next_y(i) * CORES + c)
-            cr_send(a, k, i).start()
+            c_send(a, k, next_y(i)).start()
 
         each(0, n_y - 1, one)
 
@@ -256,20 +250,12 @@
             return add(lax.rem(y + i, n_y) * CORES + c, totals)
 
         def theirs(i, totals):
-            q = next_y(i) * CORES + other
-
-            def one(k):
-                rest_arrived(a, k, q)
-                side_arrived(a, k, q)
-
-            each(1, n_ep, one)
-            return add(q, totals)
+            return add(lax.rem(y + i, n_y) * CORES + other, totals)
 
         totals = tuple(jnp.zeros((neurons, count), F32) for _ in weights)
         totals = lax.fori_loop(0, n_y, mine, totals)
-        each(1, n_ep, lambda k: arrived(a, k, y * CORES + other))
-        totals = add(y * CORES + other, totals)
-        return lax.fori_loop(0, n_y - 1, theirs, totals)
+        taken(bufs[a].at[pl.ds(0, count - rows), pl.ds(0, n_y * quarter)], r_c.at[a])
+        return lax.fori_loop(0, n_y, theirs, totals)
 
     step_cols = min(quarter, 512)
 
@@ -364,7 +350,9 @@
     each(1, n_z, lambda k: both(k, True))
     each(n_z, n_ep, lambda k: both(k, False))
     gate, upper = project(0, (wg, wu))
-    each(0, n_ep - 1, lambda i: got(wa.at[rows_at(place_of(ep_peer(i)), rows)], r_w.at[place_of(ep_peer(i))], (t, ep_peer(i))))
+    stores = [pltpu.make_async_copy(buf, ref, s_g.at[i]) for i, (buf, ref) in enumerate(((xs, x_out), (cs, c_out)))]
+    stores[0].start()
+    taken(wa.at[pl.ds(0, count - rows)], r_w)
     weight = dot(member, wa[...], ((1,), (1,)), exact)
     sig = 1.0 / (1.0 + jnp.exp(-gate))
     silu = gate * sig
@@ -374,6 +362,7 @@
     each(1, n_ep, lambda k: across(1, k))
     reduce_core(0)
     (value,) = project(1, (wd,))
+    stores[1].start()
     d_hidden = weight * value
     d_gate = d_hidden * upper * (sig * (1.0 + gate * (1.0 - sig)))
     d_up = d_hidden * silu
@@ -388,95 +377,58 @@
     reduce_core(1)
     reduce_x(0)
     fr[rows_at(p, PACK)] = fs[rows_at(p, PACK)]
-    each(0, n_ep - 1, lambda i: got(fr.at[rows_at(ep_peer(i), PACK)], r_f.at[ep_peer(i)], (t, ep_peer(i))))
+    taken(fr.at[pl.ds(0, (n_ep - 1) * PACK)], r_f)
     slot_ids = lax.broadcasted_iota(jnp.int32, (n_ep * PACK, LANES), 1).astype(F32) + 1.0
     chosen = jnp.where(fr[:, 3 * count :].astype(F32) == slot_ids, 1.0, 0.0)
     placing = chosen.T.astype(BF16)[:slots]
-    placed = dot(placing, fr[:, : 3 * count], ((1,), (0,))).astype(BF16)
-
-    keep = grads.shape[0]
-    stores = []
-    for index, wide, ref in ((1, xs, grad_gate), (2, xs, grad_up), (0, cs, grad_down)):
-        slot = len(stores) % keep
-        if len(stores) >= keep:
-            stores[len(stores) - keep].wait()
-        factor = placed[:, index * count : (index + 1) * count]
-
-        def gradient(j):
-            span = pl.ds(pl.multiple_of(j * step_cols, LANES), step_cols)
-            grads[slot, :, span] = dot(factor, wide[:, span], ((1,), (0,))).astype(BF16)
-
-        each(0, width // step_cols, gradient)
-        stores.append(pltpu.make_async_copy(grads.at[slot], ref, s_g.at[len(stores)]))
-        stores[-1].start()
+    placed[...] = dot(placing, fr[:, : 3 * count], ((1,), (0,))).astype(BF16)
+    for a in range(2):
+        fetched = pl.ds(0, quarter + (n_y - 1) * side)
+        taken(bufs[a].at[pl.ds(0, (n_z - 1) * rows), fetched], s_z.at[a])
+        taken(bufs[a].at[pl.ds(0, n_z * (n_x - 1) * rows), fetched], s_x.at[a])
+        taken(bufs[a].at[pl.ds(0, count - rows), pl.ds(0, (n_y - 1) * (quarter - side))], s_y.at[a])
+        taken(bufs[a].at[pl.ds(0, count - rows), pl.ds(0, n_y * quarter)], s_c.at[a])
+    taken(wa.at[pl.ds(0, count - rows)], s_w)
+    taken(fs.at[pl.ds(0, (n_ep - 1) * PACK)], s_f)
+    taken(sw.at[pl.ds(0, count - rows)], s_s)
     reduce_y(1)
-    each(0, n_ep - 1, lambda i: got(rw.at[ep_peer(i)], r_s.at[ep_peer(i)], (t, ep_peer(i))))
+    taken(rw.at[pl.ds(0, n_ep - 1)], r_s)
     rv[t] = jnp.sum(rw[...], 0)
     each(0, n_tp - 1, lambda i: v_send(i).start())
     reduce_x(1)
     reduce_z(0, out)
 
-    def v_got(i):
-        source = lax.rem(t + 1 + i, n_tp)
-        got(rv.at[source], r_v.at[source], (source, p))
-
-    each(0, n_tp - 1, v_got)
+    taken(rv.at[pl.ds(0, n_tp - 1)], r_v)
     per_expert = jnp.sum(rv[...], 0)
-    choice = lax.broadcasted_iota(jnp.int32, dwt.shape, 1)
-    picked = jnp.zeros(dwt.shape, F32)
-    for k in range(ce.shape[1]):
-        value_k = jnp.sum(jnp.where(ce[:, k : k + 1] == experts, per_expert, 0.0), 1, keepdims=True)
+    choice = lax.broadcasted_iota(jnp.int32, (rows, top), 1)
+    picked = jnp.zeros((rows, top), F32)
+    for k in range(top):
+        value_k = jnp.sum(jnp.where(chosen_by[:, k : k + 1] == experts, per_expert, 0.0), 1, keepdims=True)
         picked = picked + jnp.where(choice == k, value_k, 0.0)
-    dwt[...] = picked
+    dwt[...] = picked.T
     reduce_z(1, dtok)
-    for store in stores[-keep:]:
-        store.wait()
-    each(0, n_ep - 1, lambda i: w_send(i).wait_send())
-    each(0, n_ep - 1, lambda i: f_send(i).wait_send())
-    each(0, n_ep - 1, lambda i: s_send(i).wait_send())
-    each(0, n_tp - 1, lambda i: v_send(i).wait_send())
-    for a in range(2):
-        each(0, n_z - 1, lambda i: z_send(a, i).wait_send())
-        each(0, n_z - 1, lambda i: each(0, n_y - 1, lambda j: zs_send(a, i, j).wait_send()))
-
-        def row_sent(k):
-            def one(i):
-                x_send(a, k, i).wait_send()
-                each(0, n_y - 1, lambda j: xs_send(a, k, i, j).wait_send())
-
-            each(0, n_x - 1, one)
-
-        def block_sent(k):
-            def one(i):
-                y_send(a, k, i).wait_send()
-                cr_send(a, k, i).wait_send()
-                cs_send(a, k, i).wait_send()
-
-            c_send(a, k).wait_send()
-            each(0, n_y - 1, one)
-
-        each(0, n_z, row_sent)
-        each(1, n_ep, block_sent)
-        each(0, n_y, lambda q: each(0, n_x, lambda g: rc_send(a, q, g).wait_send()))
-        each(0, n_y - 1, lambda i: each(0, n_x, lambda g: ry_send(a, i, g).wait_send()))
-        each(0, n_x - 1, lambda i: rx_send(a, i).wait_send())
-        each(0, n_z - 1, lambda i: rz_send(a, i).wait_send())
-
-
-def hand_on(*refs):
-    arrays, sems = refs[:-1], refs[-1]
-    half = len(arrays) // 2
-    small, large = slice(0, 3), slice(3, half)
-    stores = [
-        pltpu.make_async_copy(src, dst, sems.at[i])
-        for i, (src, dst) in enumerate(zip(arrays[:half][large], arrays[half:][large]))
-    ]
-    for store in stores:
-        store.start()
-    for src, dst in zip(arrays[:half][small], arrays[half:][small]):
-        dst[...] = src[...]
     for store in stores:
         store.wait()
+    taken(rv.at[pl.ds(0, n_tp - 1)], s_v)
+    for a in range(2):
+        taken(part.at[a, pl.ds(0, n_y)], s_rc.at[a])
+        taken(part.at[a, pl.ds(0, n_y - 1)], s_ry.at[a])
+        taken(part.at[a, 0, pl.ds(0, (n_x - 1) * group)], s_rx.at[a])
+        taken(part.at[a, 0, pl.ds(0, (n_z - 1) * rows)], s_rz.at[a])
+
+
+def gradients(out, dtok, dwt, placed, x, c, out_to, dtok_to, dwt_to, grad_gate, grad_up, grad_down):
+    count = x.shape[0]
+
+    @pl.when(pl.program_id(0) == 0)
+    def hand_on():
+        out_to[...] = out[...]
+        dtok_to[...] = dtok[...]
+        dwt_to[...] = dwt[...]
+
+    for index, wide, grad in ((1, x, grad_gate), (2, x, grad_up), (0, c, grad_down)):
+        factor = placed[:, index * count : (index + 1) * count]
+        grad[...] = dot(factor, wide[...], ((1,), (0,))).astype(BF16)
 
 
 def body(tokens, cotangent, w_gate, w_up, w_down, neuron_expert, neuron_slot, choice_expert, choice_weight):
@@ -492,18 +444,18 @@
     slots = E_DEV * capacity
     assert peer_slots <= PACK and slots <= LANES and E_DEV * n_ep <= LANES
 
-    keep = 3 if count <= 2 * LANES else 2
     vmem = pl.BlockSpec(memory_space=pltpu.VMEM)
     anywhere = pl.BlockSpec(memory_space=pl.ANY)
     dma = pltpu.SemaphoreType.DMA
     small = jax.ShapeDtypeStruct((rows, quarter), BF16)
     grad = jax.ShapeDtypeStruct((slots, width), BF16)
-    shapes = (small, small, jax.ShapeDtypeStruct(choice_weight.shape, F32), grad, grad, grad)
+    wide = jax.ShapeDtypeStruct((count, width), BF16)
+    direct = (small, small, jax.ShapeDtypeStruct(choice_weight.shape[::-1], F32))
     results = pl.pallas_call(
         functools.partial(kernel, n_tp, n_ep),
-        out_shape=shapes,
+        out_shape=direct + (jax.ShapeDtypeStruct((slots, 3 * count), BF16), wide, wide),
         in_specs=[vmem] * 9,
-        out_specs=[vmem] * 3 + [anywhere] * 3,
+        out_specs=[vmem] * 4 + [anywhere] * 2,
         scratch_shapes=[
             pltpu.VMEM((count, width), BF16),
             pltpu.VMEM((count, width), BF16),
@@ -518,48 +470,50 @@
             pltpu.VMEM((2, n_y - 1, n_x, group, quarter), BF16),
             pltpu.VMEM((2, n_x, group, quarter), BF16),
             pltpu.VMEM((2, n_z, rows, quarter), BF16),
-            pltpu.VMEM((keep, slots, width), BF16),
-            dma((2, n_z)),
-            dma((2, n_z, n_y)),
-            dma((2, n_z, n_x)),
-            dma((2, n_z, n_x, n_y)),
-            dma((2, n_ep, n_y)),
-            dma((2, n_ep, n_y)),
-            dma((2, n_ep, n_y)),
+            dma((2,)),
+            dma((2,)),
+            dma((2,)),
+            dma((2,)),
             dma((2, n_ep, n_tp)),
             dma((2, n_ep, n_tp)),
-            dma((n_ep,)),
-            dma((n_ep,)),
-            dma((n_ep,)),
-            dma((n_ep,)),
-            dma((n_ep,)),
-            dma((n_ep,)),
-            dma((n_tp,)),
-            dma((n_tp,)),
+            dma((2,)),
+        ]
+        + [dma] * 8
+        + [
+            dma((2,)),
             dma((2, n_y, n_x)),
+            dma((2,)),
             dma((2, n_y, n_x)),
-            dma((2, n_y, n_x)),
-            dma((2, n_y, n_x)),
+            dma((2,)),
             dma((2, n_x)),
-            dma((2, n_x)),
+            dma((2,)),
             dma((2, n_z)),
-            dma((2, n_z)),
-            dma((3,)),
+            dma((2,)),
         ],
         compiler_params=pltpu.CompilerParams(
             collective_id=0, has_side_effects=True, vmem_limit_bytes=62 * 1024 * 1024
         ),
     )(
         tokens, cotangent, w_gate, w_up, w_down,
-        neuron_expert.reshape(1, -1), neuron_slot.reshape(1, -1), choice_expert, choice_weight,
+        neuron_expert.reshape(1, -1), neuron_slot.reshape(1, -1), choice_expert.T, choice_weight.T,
     )
+    chunk = min(width, 8 * LANES)
+
+    def whole(ref):
+        return pl.BlockSpec(ref.shape, lambda j: (0, 0))
+
+    def columns(height):
+        return pl.BlockSpec((height, chunk), lambda j: (0, j))
+
     output, d_tokens, d_weight, d_gate, d_up, d_down = pl.pallas_call(
-        hand_on,
-        out_shape=shapes,
-        in_specs=[vmem] * 3 + [anywhere] * 3,
-        out_specs=[vmem] * 3 + [anywhere] * 3,
-        scratch_shapes=[dma((3,))],
+        gradients,
+        grid=(width // chunk,),
+        out_shape=direct + (grad, grad, grad),
+        in_specs=[whole(ref) for ref in results[:4]] + [columns(count)] * 2,
+        out_specs=[whole(ref) for ref in direct] + [columns(slots)] * 3,
+        compiler_params=pltpu.CompilerParams(vmem_limit_bytes=62 * 1024 * 1024),
     )(*results)
+    d_weight = d_weight.T
 
     def expert_blocks(rows_):
         return rows_.reshape(E_DEV, capacity, width)

time: 252 us -> 80.9 us (0.32)
  Pallas kernels: 247 us -> 80 us
  local copies, waits for them, and re-layouts: 4.07 us -> 0 us
    pallas_call x2, Pallas kernels: 247 us -> 80 us  [the longest x1 72.6 us: body(): pl.pallas_call(functools.partial(kernel, n_tp, n_ep), out_shape=direct +...]
    unnamed x3 -> x0, local copies, waits for them, and re-layouts: 4.07 us -> none
where the time goes in v4:
time: 80.9 us; the launch traced here: 80.6 us
  Pallas kernels  80 us (99%)
    pallas_call x1, Pallas kernels, body(): pl.pallas_call(functools.partial(kernel, n_tp, n_ep), out_shape=direct +...  72.6 us
    pallas_call x1, Pallas kernels, body(): pl.pallas_call(gradients, grid=(width // chunk,), out_shape=direct + (gra...  7.42 us

profile of v4, /device:TPU:0, one launch (start us, length us, event | category | flops | bytes accessed | tf_op | source)
XLA Modules:
  0.0 80.6 jit_solution(274955112267705954)
XLA Ops:
  0.6 72.6 %shard_map.136 = (bf16[16,2048]{1,0:T(8,128)(2,1)}, bf16[16,2048]{1,0:T(8,128)(2,1)}, f32[8,16]{1,0:T(8,128)}, bf16[112,384]{1,0:T(8,128)(2,1)}, bf16[128,8192]{1,0:T(8,128)(2,1)}, /*index=5*/bf16[128,8192]{1,0:T(8,128)(2,1)}) custom-call(bf16[16,8192]{1,0:T(8,128)(2,1)} %tok.1, bf16[16,8192]{1,0:T(8,128)(2,1)} %cot.1, bf16[56,8192]{1,0:T(8,128)(2,1)} %wg.1, ...), custom_call_target="tpu_custom_call" | custom-call | tf_op jit(solution)/shard_map/pallas_call | solution.py:454
  73.2 7.4 %shard_map.137 = (bf16[16,2048]{1,0:T(8,128)(2,1)}, bf16[16,2048]{1,0:T(8,128)(2,1)}, f32[8,16]{1,0:T(8,128)}, bf16[112,8192]{1,0:T(8,128)(2,1)}, bf16[112,8192]{1,0:T(8,128)(2,1)}, /*index=5*/bf16[112,8192]{1,0:T(8,128)(2,1)}) custom-call(bf16[16,2048]{1,0:T(8,128)(2,1)} %get-tuple-element.18.out, bf16[16,2048]{1,0:T(8,128)(2,1)} %get-tuple-element.19.dtok, ...), custom_call_target="tpu_custom_call" | custom-call | tf_op jit(solution)/shard_map/pallas_call | solution.py:508

commit v5 on v4

--- a/solution.py
+++ b/solution.py
@@ -40,9 +40,9 @@
 def kernel(
     n_tp, n_ep, tok, cot, wg, wu, wd, ne, ns, ce, cw,
     out, dtok, dwt, placed, x_out, c_out,
-    xs, cs, wa, fs, fr, sw, rw, rv, part, rc, ry, rx, rz,
+    xs, cs, wa, fs, fr, sw, rw, rv, part, shared, stack, crossing, ry, rx, rz,
     s_z, s_x, s_y, s_c, r_ag, r_sd, r_c, s_w, r_w, s_f, r_f, s_s, r_s, s_v, r_v,
-    s_rc, r_rc, s_ry, r_ry, s_rx, r_rx, s_rz, r_rz, s_g,
+    s_wt, r_wt, s_fx, r_fx, s_ry, r_ry, s_rx, r_rx, s_rz, r_rz, s_g,
 ):
     n_y, n_z, n_x = grid_of(n_tp, n_ep)
     t, p = lax.axis_index("tp"), lax.axis_index("ep")
@@ -156,23 +156,30 @@
         to = lax.rem(t + 1 + i, n_tp)
         return copy(rv.at[t], rv.at[t], s_v, r_v, (to, p))
 
-    def rc_send(a, qy, g):
-        src = part.at[a, qy * CORES + other, rows_at(g, group)]
-        return copy(src, rc.at[a, qy, g], s_rc.at[a], r_rc.at[a, qy, g], (y * CORES + other, p))
+    high = shared.shape[1] // 3
+
+    def wt_send(qy, w):
+        src = shared.at[qy, pl.ds(w * high, high)]
+        dst = stack.at[qy, rows_at(w * CORES + c, high)]
+        return copy(src, dst, s_wt, r_wt, sibling)
+
+    def fx_send(w):
+        ref = crossing.at[rows_at(w * CORES + c, high)]
+        return copy(ref, ref, s_fx.at[w], r_fx.at[w], sibling)
 
     def ry_send(a, i, g):
-        to = lax.rem(y + 1 + i, n_y) * CORES + c
-        src = part.at[a, to, rows_at(g, group)]
+        to = next_y(i) * CORES + c
+        src = part.at[a, next_y(i), rows_at(g, group)]
         return copy(src, ry.at[a, n_y - 2 - i, g], s_ry.at[a], r_ry.at[a, n_y - 2 - i, g], (to, p))
 
     def rx_send(a, i):
         to = lax.rem(x + 1 + i, n_x)
-        src = part.at[a, t, rows_at(to, group)]
+        src = part.at[a, y, rows_at(to, group)]
         return copy(src, rx.at[a, x], s_rx.at[a], r_rx.at[a, x], at(z, to))
 
     def rz_send(a, i):
         to = lax.rem(z + 1 + i, n_z)
-        src = part.at[a, t, rows_at(place(to, x), rows)]
+        src = part.at[a, y, rows_at(place(to, x), rows)]
         return copy(src, rz.at[a, z], s_rz.at[a], r_rz.at[a, z], at(to, x))
 
     barrier = pltpu.get_barrier_semaphore()
@@ -191,6 +198,18 @@
         each(0, n_z - 1, lambda i: each(0, n_y - 1, lambda j: zs_send(a, i, j).start()))
         each(0, n_x - 1, lambda i: each(0, n_y - 1, lambda j: xs_send(a, 0, i, j).start()))
 
+    held = wg.shape[0]
+    blank = jnp.zeros((high - held, quarter), BF16)
+    for w, weight in enumerate((wd, wg, wu)):
+
+        def lay(qy):
+            shared[qy, w * high : w * high + held] = weight[:, cols_at(qy * CORES + other)]
+            shared[qy, w * high + held : (w + 1) * high] = blank
+            wt_send(qy, w).start()
+            own = pl.multiple_of((w * CORES + c) * high, high)
+            stack[qy, pl.ds(own, high)] = jnp.concatenate([weight[:, cols_at(qy * CORES + c)], blank], 0)
+
+        each(0, n_y, lay)
     experts = lax.broadcasted_iota(jnp.int32, (rows, LANES), 1).astype(F32)
     by_expert = jnp.zeros((rows, LANES), F32)
     chosen_by, weight_by = ce[...].astype(F32).T, cw[...].T
@@ -201,7 +220,7 @@
     each(0, n_ep - 1, lambda i: w_send(i).start())
 
     neurons = wg.shape[0]
-    slots = placed.shape[0]
+    slots = placed.shape[0] // 3
     named = ne[...]
     owner = lax.div(named, E_DEV)
 
@@ -259,25 +278,30 @@
 
     step_cols = min(quarter, 512)
 
-    def spread(a, pairs):
-        def one(q):
+    def hand(w, factor):
+        pad = jnp.zeros((high - neurons, count), F32)
+        crossing[rows_at(w * CORES + c, high)] = jnp.concatenate([factor, pad], 0)
+        fx_send(w).start()
+
+    def spread(a, low, tall):
+        for w in range(low, low + tall):
+            got(crossing.at[rows_at(w * CORES + other, high)], r_fx.at[w], sibling)
+        span = slice(low * CORES * high, (low + tall) * CORES * high)
+        factor = crossing[span].T.astype(BF16)
+
+        def one(qy):
             def chunk(j):
-                at_cols = pl.ds(pl.multiple_of(q * quarter + j * step_cols, LANES), step_cols)
-                total = None
-                for factor, weight in pairs:
-                    term = dot(factor, weight[:, at_cols], ((1,), (0,)))
-                    total = term if total is None else total + term
-                part[a, q, :, pl.ds(pl.multiple_of(j * step_cols, LANES), step_cols)] = total.astype(BF16)
+                at_cols = pl.ds(pl.multiple_of(j * step_cols, LANES), step_cols)
+                part[a, qy, :, at_cols] = dot(factor, stack[qy, span, at_cols], ((1,), (0,))).astype(BF16)
 
             each(0, quarter // step_cols, chunk)
 
         def away(i):
-            qy = lax.rem(y + 1 + i, n_y)
-            one(qy * CORES + other)
-            each(0, n_x, lambda g: rc_send(a, qy, lax.rem(x + 1 + g, n_x)).start())
-
-        each(0, n_y, away)
-        each(0, n_y, lambda i: one(lax.rem(y + 1 + i, n_y) * CORES + c))
+            one(next_y(i))
+            each(0, n_x, lambda g: ry_send(a, i, lax.rem(x + 1 + g, n_x)).start())
+
+        each(0, n_y - 1, away)
+        one(y)
 
     def add_into(a, q, base, ref):
         def some(j):
@@ -288,30 +312,12 @@
 
         each(0, ref.shape[0] // rows, some)
 
-    def reduce_core(a):
-        def one(gi):
-            g = lax.rem(x + 1 + gi, n_x)
-
-            def turn(i):
-                qy = lax.rem(y + 1 + i, n_y)
-                got(rc.at[a, qy, g], r_rc.at[a, qy, g], (y * CORES + other, p))
-                add_into(a, qy * CORES + c, g * n_z, rc.at[a, qy, g])
-
-            def send(i):
-                turn(i)
-                ry_send(a, i, g).start()
-
-            each(0, n_y - 1, send)
-            turn(n_y - 1)
-
-        each(0, n_x, one)
-
     def reduce_y(a):
         def one(g):
             def add(i):
                 qy = lax.rem(y + 1 + i, n_y)
                 got(ry.at[a, i, g], r_ry.at[a, i, g], (qy * CORES + c, p))
-                add_into(a, t, g * n_z, ry.at[a, i, g])
+                add_into(a, y, g * n_z, ry.at[a, i, g])
 
             each(0, n_y - 1, add)
 
@@ -326,13 +332,13 @@
         def add(i):
             from_x = lax.rem(x + 1 + i, n_x)
             got(rx.at[a, from_x], r_rx.at[a, from_x], at(z, from_x))
-            add_into(a, t, x * n_z, rx.at[a, from_x])
+            add_into(a, y, x * n_z, rx.at[a, from_x])
 
         each(0, n_x - 1, add)
         each(0, n_z - 1, lambda i: rz_send(a, i).start())
 
     def reduce_z(a, result):
-        total = part[a, t, rows_at(here, rows)].astype(F32)
+        total = part[a, y, rows_at(here, rows)].astype(F32)
         for i in range(n_z - 1):
             from_z = lax.rem(z + 1 + i, n_z)
             got(rz.at[a, from_z], r_rz.at[a, from_z], at(from_z, x))
@@ -358,30 +364,33 @@
     silu = gate * sig
     hidden = silu * upper
     scaled = weight * hidden
-    spread(0, [(scaled.T.astype(BF16), wd)])
+    hand(0, scaled)
     each(1, n_ep, lambda k: across(1, k))
-    reduce_core(0)
+    taken(stack.at[pl.ds(0, n_y), pl.ds(0, 3 * high)], r_wt)
+    spread(0, 0, 1)
     (value,) = project(1, (wd,))
     stores[1].start()
     d_hidden = weight * value
     d_gate = d_hidden * upper * (sig * (1.0 + gate * (1.0 - sig)))
     d_up = d_hidden * silu
+    hand(1, d_gate)
+    hand(2, d_up)
     factors = jnp.concatenate([scaled.astype(BF16), d_gate.astype(BF16), d_up.astype(BF16), label], 1)
     fs[...] = dot(pack, factors, ((1,), (0,))).astype(BF16)
     each(0, n_ep - 1, lambda i: f_send(i).start())
-    spread(1, [(d_gate.T.astype(BF16), wg), (d_up.T.astype(BF16), wu)])
+    spread(1, 1, 2)
     reduce_y(0)
     sw[...] = dot((hidden * value).T, member, ((1,), (0,)), exact)
     each(0, n_ep - 1, lambda i: s_send(i).start())
     rw[p] = sw[rows_at(here, rows)]
-    reduce_core(1)
     reduce_x(0)
     fr[rows_at(p, PACK)] = fs[rows_at(p, PACK)]
     taken(fr.at[pl.ds(0, (n_ep - 1) * PACK)], r_f)
     slot_ids = lax.broadcasted_iota(jnp.int32, (n_ep * PACK, LANES), 1).astype(F32) + 1.0
     chosen = jnp.where(fr[:, 3 * count :].astype(F32) == slot_ids, 1.0, 0.0)
     placing = chosen.T.astype(BF16)[:slots]
-    placed[...] = dot(placing, fr[:, : 3 * count], ((1,), (0,))).astype(BF16)
+    for i in range(3):
+        placed[i * slots : (i + 1) * slots] = dot(placing, fr[:, i * count : (i + 1) * count], ((1,), (0,))).astype(BF16)
     for a in range(2):
         fetched = pl.ds(0, quarter + (n_y - 1) * side)
         taken(bufs[a].at[pl.ds(0, (n_z - 1) * rows), fetched], s_z.at[a])
@@ -411,24 +420,26 @@
         store.wait()
     taken(rv.at[pl.ds(0, n_tp - 1)], s_v)
     for a in range(2):
-        taken(part.at[a, pl.ds(0, n_y)], s_rc.at[a])
         taken(part.at[a, pl.ds(0, n_y - 1)], s_ry.at[a])
         taken(part.at[a, 0, pl.ds(0, (n_x - 1) * group)], s_rx.at[a])
         taken(part.at[a, 0, pl.ds(0, (n_z - 1) * rows)], s_rz.at[a])
+    for w in range(3):
+        taken(crossing.at[pl.ds(0, high)], s_fx.at[w])
+    taken(shared, s_wt)
 
 
 def gradients(out, dtok, dwt, placed, x, c, out_to, dtok_to, dwt_to, grad_gate, grad_up, grad_down):
-    count = x.shape[0]
-
     @pl.when(pl.program_id(0) == 0)
     def hand_on():
         out_to[...] = out[...]
         dtok_to[...] = dtok[...]
         dwt_to[...] = dwt[...]
 
-    for index, wide, grad in ((1, x, grad_gate), (2, x, grad_up), (0, c, grad_down)):
-        factor = placed[:, index * count : (index + 1) * count]
-        grad[...] = dot(factor, wide[...], ((1,), (0,))).astype(BF16)
+    slots = grad_down.shape[0]
+    grad_down[...] = dot(placed[:slots], c[...], ((1,), (0,))).astype(BF16)
+    both = dot(placed[slots:], x[...], ((1,), (0,))).astype(BF16)
+    grad_gate[...] = both[:slots]
+    grad_up[...] = both[slots:]
 
 
 def body(tokens, cotangent, w_gate, w_up, w_down, neuron_expert, neuron_slot, choice_expert, choice_weight):
@@ -439,6 +450,7 @@
     count = n_ep * rows
     quarter = width // n_tp
     group = n_z * rows
+    high = -(-neurons // PACK) * PACK
     peer_slots = 2 * ((neurons + n_ep - 1) // n_ep)
     capacity = n_ep * peer_slots // E_DEV
     slots = E_DEV * capacity
@@ -453,7 +465,7 @@
     direct = (small, small, jax.ShapeDtypeStruct(choice_weight.shape[::-1], F32))
     results = pl.pallas_call(
         functools.partial(kernel, n_tp, n_ep),
-        out_shape=direct + (jax.ShapeDtypeStruct((slots, 3 * count), BF16), wide, wide),
+        out_shape=direct + (jax.ShapeDtypeStruct((3 * slots, count), BF16), wide, wide),
         in_specs=[vmem] * 9,
         out_specs=[vmem] * 4 + [anywhere] * 2,
         scratch_shapes=[
@@ -465,8 +477,10 @@
             pltpu.VMEM((count, LANES), F32),
             pltpu.VMEM((n_ep, rows, LANES), F32),
             pltpu.VMEM((n_tp, rows, LANES), F32),
-            pltpu.VMEM((2, n_tp, count, quarter), BF16),
-            pltpu.VMEM((2, n_y, n_x, group, quarter), BF16),
+            pltpu.VMEM((2, n_y, count, quarter), BF16),
+            pltpu.VMEM((n_y, 3 * high, quarter), BF16),
+            pltpu.VMEM((n_y, 3 * CORES * high, quarter), BF16),
+            pltpu.VMEM((3 * CORES * high, count), F32),
             pltpu.VMEM((2, n_y - 1, n_x, group, quarter), BF16),
             pltpu.VMEM((2, n_x, group, quarter), BF16),
             pltpu.VMEM((2, n_z, rows, quarter), BF16),
@@ -480,8 +494,10 @@
         ]
         + [dma] * 8
         + [
-            dma((2,)),
-            dma((2, n_y, n_x)),
+            dma,
+            dma,
+            dma((3,)),
+            dma((3,)),
             dma((2,)),
             dma((2, n_y, n_x)),
             dma((2,)),
@@ -497,7 +513,7 @@
         tokens, cotangent, w_gate, w_up, w_down,
         neuron_expert.reshape(1, -1), neuron_slot.reshape(1, -1), choice_expert.T, choice_weight.T,
     )
-    chunk = min(width, 8 * LANES)
+    chunk = min(width, 16 * LANES)
 
     def whole(ref):
         return pl.BlockSpec(ref.shape, lambda j: (0, 0))

time: 80.9 us -> 79 us (0.977)
  Pallas kernels: 80 us -> 78.2 us
    pallas_call x1, Pallas kernels: 7.42 us -> 5.91 us  [body(): pl.pallas_call(gradients, grid=(width // chunk,), out_shape=direct + (gra...]
where the time goes in v5:
time: 79 us; the launch traced here: 78.8 us
  Pallas kernels  78.2 us (99%)
    pallas_call x1, Pallas kernels, body(): pl.pallas_call(functools.partial(kernel, n_tp, n_ep), out_shape=direct +...  72.2 us
    pallas_call x1, Pallas kernels, body(): pl.pallas_call(gradients, grid=(width // chunk,), out_shape=direct + (gra...  5.91 us

profile of v5, /device:TPU:0, one launch (start us, length us, event | category | flops | bytes accessed | tf_op | source)
XLA Modules:
  0.0 78.8 jit_solution(10403129730650638617)
XLA Ops:
  0.6 72.2 %shard_map.136 = (bf16[16,2048]{1,0:T(8,128)(2,1)}, bf16[16,2048]{1,0:T(8,128)(2,1)}, f32[8,16]{1,0:T(8,128)}, bf16[336,128]{1,0:T(8,128)(2,1)}, bf16[128,8192]{1,0:T(8,128)(2,1)}, /*index=5*/bf16[128,8192]{1,0:T(8,128)(2,1)}) custom-call(bf16[16,8192]{1,0:T(8,128)(2,1)} %tok.1, bf16[16,8192]{1,0:T(8,128)(2,1)} %cot.1, bf16[56,8192]{1,0:T(8,128)(2,1)} %wg.1, ...), custom_call_target="tpu_custom_call" | custom-call | tf_op jit(solution)/shard_map/pallas_call | solution.py:466
  72.9 5.9 %shard_map.137 = (bf16[16,2048]{1,0:T(8,128)(2,1)}, bf16[16,2048]{1,0:T(8,128)(2,1)}, f32[8,16]{1,0:T(8,128)}, bf16[112,8192]{1,0:T(8,128)(2,1)}, bf16[112,8192]{1,0:T(8,128)(2,1)}, /*index=5*/bf16[112,8192]{1,0:T(8,128)(2,1)}) custom-call(bf16[16,2048]{1,0:T(8,128)(2,1)} %get-tuple-element.18.out, bf16[16,2048]{1,0:T(8,128)(2,1)} %get-tuple-element.19.dtok, ...), custom_call_target="tpu_custom_call" | custom-call | tf_op jit(solution)/shard_map/pallas_call | solution.py:524

commit v6 on v5

--- a/solution.py
+++ b/solution.py
@@ -192,11 +192,13 @@
     cs[rows_at(here, rows)] = cot[...]
     pl.semaphore_wait(barrier, n_ep - 1 + n_tp - 1)
 
-    for a in range(2):
+    def open_with(a):
         each(0, n_z - 1, lambda i: z_send(a, i).start())
         each(0, n_x - 1, lambda i: x_send(a, 0, i).start())
         each(0, n_z - 1, lambda i: each(0, n_y - 1, lambda j: zs_send(a, i, j).start()))
         each(0, n_x - 1, lambda i: each(0, n_y - 1, lambda j: xs_send(a, 0, i, j).start()))
+
+    open_with(0)
 
     held = wg.shape[0]
     blank = jnp.zeros((high - held, quarter), BF16)
@@ -347,14 +349,10 @@
 
     exact = lax.Precision.HIGHEST
     each(1, n_z, lambda k: forward(0, k, True))
+    open_with(1)
     each(n_z, n_ep, lambda k: forward(0, k, False))
-
-    def both(k, near):
-        across(0, k)
-        forward(1, k, near)
-
-    each(1, n_z, lambda k: both(k, True))
-    each(n_z, n_ep, lambda k: both(k, False))
+    each(1, n_ep, lambda k: across(0, k))
+    each(1, n_z, lambda k: forward(1, k, True))
     gate, upper = project(0, (wg, wu))
     stores = [pltpu.make_async_copy(buf, ref, s_g.at[i]) for i, (buf, ref) in enumerate(((xs, x_out), (cs, c_out)))]
     stores[0].start()
@@ -365,9 +363,10 @@
     hidden = silu * upper
     scaled = weight * hidden
     hand(0, scaled)
-    each(1, n_ep, lambda k: across(1, k))
+    each(n_z, n_ep, lambda k: forward(1, k, False))
     taken(stack.at[pl.ds(0, n_y), pl.ds(0, 3 * high)], r_wt)
     spread(0, 0, 1)
+    each(1, n_ep, lambda k: across(1, k))
     (value,) = project(1, (wd,))
     stores[1].start()
     d_hidden = weight * value

time: 79 us -> 73.7 us (0.933)
  Pallas kernels: 78.2 us -> 72.9 us
    pallas_call x1, Pallas kernels: 72.2 us -> 66.9 us  [body(): pl.pallas_call(functools.partial(kernel, n_tp, n_ep), out_shape=direct +...]
where the time goes in v6:
time: 73.7 us; the launch traced here: 73.5 us
  Pallas kernels  72.9 us (99%)
    pallas_call x1, Pallas kernels, body(): pl.pallas_call(functools.partial(kernel, n_tp, n_ep), out_shape=direct +...  66.9 us
    pallas_call x1, Pallas kernels, body(): pl.pallas_call(gradients, grid=(width // chunk,), out_shape=direct + (gra...  5.91 us

profile of v6, /device:TPU:0, one launch (start us, length us, event | category | flops | bytes accessed | tf_op | source)
XLA Modules:
  0.0 73.5 jit_solution(7327371672057384260)
XLA Ops:
  0.6 66.9 %shard_map.136 = (bf16[16,2048]{1,0:T(8,128)(2,1)}, bf16[16,2048]{1,0:T(8,128)(2,1)}, f32[8,16]{1,0:T(8,128)}, bf16[336,128]{1,0:T(8,128)(2,1)}, bf16[128,8192]{1,0:T(8,128)(2,1)}, /*index=5*/bf16[128,8192]{1,0:T(8,128)(2,1)}) custom-call(bf16[16,8192]{1,0:T(8,128)(2,1)} %tok.1, bf16[16,8192]{1,0:T(8,128)(2,1)} %cot.1, bf16[56,8192]{1,0:T(8,128)(2,1)} %wg.1, ...), custom_call_target="tpu_custom_call" | custom-call | tf_op jit(solution)/shard_map/pallas_call | solution.py:465
  67.6 5.9 %shard_map.137 = (bf16[16,2048]{1,0:T(8,128)(2,1)}, bf16[16,2048]{1,0:T(8,128)(2,1)}, f32[8,16]{1,0:T(8,128)}, bf16[112,8192]{1,0:T(8,128)(2,1)}, bf16[112,8192]{1,0:T(8,128)(2,1)}, /*index=5*/bf16[112,8192]{1,0:T(8,128)(2,1)}) custom-call(bf16[16,2048]{1,0:T(8,128)(2,1)} %get-tuple-element.18.out, bf16[16,2048]{1,0:T(8,128)(2,1)} %get-tuple-element.19.dtok, ...), custom_call_target="tpu_custom_call" | custom-call | tf_op jit(solution)/shard_map/pallas_call | solution.py:523
